TPU v7x, 256 devices: a whole 4x4x8 slice. The times are simulated.
256 devices in a mesh: replica: 32 (over x_hi, z, core), tensor: 8 (over x_lo, y).
Axes of the slice: x: 4 (x_hi: 2, x_lo: 2; x = x_hi * 2 + x_lo), y: 4, z: 8, core: 2. Of those that a mesh axis runs over, the one named last changes fastest.
Arguments:
- delta_codes: int32 [32, 2, 4096, 1024], P('replica', None, None, 'tensor'), may hold values from 0 to 255
- scale_exponents: int32 [32, 2, 256, 1024], P('replica', None, None, 'tensor'), may hold values from -5 to -1
- outer_params: float32 [2, 8192, 1024], P(None, 'replica', 'tensor'), may hold values from -6 to 6
- outer_momentum: float32 [2, 8192, 1024], P(None, 'replica', 'tensor'), may hold values from -4 to 4
- tensor_partials: bfloat16 [8, 12288, 8192], P('tensor', 'replica'), may hold values from -6 to 6
- residual_stream: bfloat16 [12288, 8192], P('replica', 'tensor'), may hold values from -150 to 150, as said below
- norm_gain: float32 [8192], replicated, may hold values from 0.1 to 1.9
Outputs:
- keys_values: bfloat16 [2, 12288, 1024], P(None, 'replica', 'tensor')
- params_out: float32 [2, 8192, 1024], P(None, 'replica', 'tensor')
- momentum_out: float32 [2, 8192, 1024], P(None, 'replica', 'tensor')
Inputs may be any that keep to these rules, and one draw needn't show every extreme that they name: residual_stream has rows and features of differing scales.
All inputs are finite; a program needn't handle non-finite values.
Results may differ from a plain program's by a relative error of at most 0.018.
Values may be sent and summed in bfloat16 or wider, within the bound.
A program may use at most 128 MiB of HBM per device.

v0:
```python
import jax
import jax.numpy as jnp
from jax import lax
from jax.sharding import PartitionSpec as P

D = 8192
BLOCK = 32


outer_rate = 0.7
outer_beta = 0.9
lowest_exponent = -5
norm_epsilon = 1e-05


def unpack_codes(words):
    nibbles = [jnp.bitwise_and(jnp.right_shift(words, 4 * place), 15) for place in range(2)]
    stacked = jnp.stack(nibbles, axis=2)
    return stacked.reshape(words.shape[0], words.shape[1] * 2, words.shape[2])


def decode_block(words, exponents):
    codes = unpack_codes(words)
    magnitude = codes % 8
    sign_factor = 1.0 - 2.0 * (codes // 8).astype(jnp.float32)
    exponent_bits = magnitude // 2
    mantissa = (magnitude % 2).astype(jnp.float32)
    power_part = jnp.where(exponent_bits == 3, 4.0, jnp.where(exponent_bits == 2, 2.0, 1.0))
    value = (
        jnp.where(exponent_bits == 0, 0.5 * mantissa, power_part * (1.0 + 0.5 * mantissa))
        * sign_factor
    )
    block_scale = (
        jnp.left_shift(jnp.ones_like(exponents), exponents - lowest_exponent).astype(jnp.float32)
        * 2.0**lowest_exponent
    )
    shaped = (
        value.reshape(codes.shape[0], codes.shape[1] // BLOCK, BLOCK, codes.shape[2])
        * block_scale[:, :, None, :]
    )
    return shaped.reshape(codes.shape).astype(jnp.bfloat16)


def per_device(
    delta_codes,
    scale_exponents,
    outer_params,
    outer_momentum,
    tensor_partials,
    residual_stream,
    norm_gain,
):
    decoded = decode_block(delta_codes[0], scale_exponents[0])
    replicas = lax.axis_size("replica")
    summed = lax.psum_scatter(decoded, "replica", scatter_dimension=1, tiled=True).astype(
        jnp.float32
    )
    outer_grad = summed / replicas
    momentum_out = outer_beta * outer_momentum + outer_grad
    params_out = outer_params - outer_rate * (outer_grad + outer_beta * momentum_out)
    fragment = params_out.astype(jnp.bfloat16)
    feature_sum = lax.psum_scatter(
        tensor_partials[0].astype(jnp.float32).astype(jnp.bfloat16),
        "tensor",
        scatter_dimension=1,
        tiled=True,
    ).astype(jnp.float32)
    hidden_share = (residual_stream.astype(jnp.float32) + feature_sum).astype(jnp.bfloat16)
    hidden = lax.all_gather(hidden_share, "tensor", axis=1, tiled=True)
    hidden_float = hidden.astype(jnp.float32)
    inverse = lax.rsqrt(
        jnp.mean(hidden_float * hidden_float, axis=-1, keepdims=True) + norm_epsilon
    )
    normed = (hidden_float * inverse * norm_gain).astype(jnp.bfloat16)
    projected = jnp.einsum(
        "td,jdk->jtk",
        normed,
        lax.all_gather(fragment, "replica", axis=1, tiled=True),
        preferred_element_type=jnp.float32,
    )
    keys_values = (projected * D ** (-0.5)).astype(jnp.bfloat16)
    return (keys_values, params_out, momentum_out)


def solution(mesh):
    return jax.shard_map(
        per_device,
        mesh=mesh,
        in_specs=(
            P("replica", None, None, "tensor"),
            P("replica", None, None, "tensor"),
            P(None, "replica", "tensor"),
            P(None, "replica", "tensor"),
            P("tensor", "replica", None),
            P("replica", "tensor"),
            P(),
        ),
        out_specs=(
            P(None, "replica", "tensor"),
            P(None, "replica", "tensor"),
            P(None, "replica", "tensor"),
        ),
        check_vma=False,
    )
```

profile of v0, /device:TPU:1, one launch (start us, length us, event | category | flops | bytes accessed | tf_op | source)
XLA Modules:
  0.0 398.7 jit_solution(6278133732411448192)
XLA Ops:
  7.2 0.0 reduce-scatter.5.cloned.1.call-start
  7.2 0.7 reduce-scatter.5.cloned.1.call-update
  7.9 0.0 reduce-scatter.3.cloned.1.call-start
  7.9 2.7 and_bitcast_fusion.1
  10.7 0.5 pad_add_fusion
  11.2 31.3 %copy.17 = s32[2,4096,2,128]{3,2,1,0:T(2,128)} copy(s32[2,4096,2,128]{3,1,0,2:T(8,128)S(1)} %pad_add_fusion) | data formatting | bytes 16777216 | tf_op jit(solution)/shard_map/stack | solution.py:18
  42.5 0.0 copy-start.1
  42.5 9.0 %copy.18 = s32[2,8192,128]{1,2,0:T(8,128)} copy(s32[2,8192,128]{2,1,0:T(8,128)} %bitcast.21) | data formatting | bytes 16777216 | tf_op jit(solution)/shard_map/reshape | solution.py:19
  51.5 0.0 copy-done.1
  51.6 3.8 mul.93
  55.3 9.0 %copy.22 = f32[2,8192,128]{1,2,0:T(8,128)} copy(f32[2,8192,128]{2,1,0:T(8,128)} %bitcast.22) | data formatting | bytes 16777216 | tf_op jit(solution)/shard_map/mul | solution.py:38
  64.3 0.0 copy-start
  64.3 0.0 copy-start.2
  64.3 0.0 copy-start.3
  64.3 21.6 %fusion.10 = bf16[2,8192,128]{1,2,0:T(8,128)(2,1)} fusion(f32[2,8192,128]{1,2,0:T(8,128)} %copy.22, s32[2,8192,128]{1,2,0:T(8,128)} %copy.18), kind=kLoop, calls=%fused_computation.22 | loop fusion | flops 113246208 | bytes 20971520 | tf_op jit(solution)/shard_map/convert_element_type | solution.py:41
  85.9 0.0 copy-start.4
  85.9 0.0 reduce-scatter.3.cloned.1.call-update
  85.9 0.2 all-gather.5.cloned.1.call-start
  86.2 3.7 reduce-scatter.5.cloned.1.call-done
  89.9 0.0 copy-done
  89.9 2.3 add_convert_fusion
  92.2 0.0 all-gather.5.cloned.1.call-update
  92.2 0.0 all-gather.3.cloned.1.call-start
  92.3 0.0 copy-done.2
  92.3 0.1 copy.23
  92.4 0.0 copy-done.3
  92.4 0.1 copy.24
  92.6 123.7 %reduce-scatter.3.cloned.1.call-done = bf16[2,256,128]{1,2,0:T(8,128)(2,1)} async-done(((bf16[2,8192,128]{1,2,0:T(8,128)(2,1)}), bf16[2,256,128]{1,2,0:T(8,128)(2,1)}) %reduce-scatter.3.cloned.1.call-update) | async-done | bytes 131088 | tf_op jit(solution)/shard_map/reduce_scatter | solution.py:55
  216.2 1.6 fusion.26
  217.9 0.0 all-gather.3.cloned.1.call-update
  217.9 0.8 copy.26
  218.7 0.8 copy.27
  219.6 75.7 %all-gather.5.cloned.1.call-done = bf16[384,8192]{1,0:T(8,128)(2,1)} async-done(((bf16[384,1024]{1,0:T(8,128)(2,1)}), bf16[384,8192]{1,0:T(8,128)(2,1)}) %all-gather.5.cloned.1.call-update) | async-done | bytes 6291472 | tf_op jit(solution)/shard_map/all_gather | solution.py:69
  295.2 4.1 %fusion = f32[384]{0:T(512)S(1)} fusion(bf16[384,8192]{1,0:T(8,128)(2,1)} %all-gather.5.cloned.1.call-done), kind=kLoop, calls=%fused_computation.2 | loop fusion | flops 9436800 | bytes 6292992 | tf_op jit(solution)/shard_map/reduce_sum | solution.py:72
  299.4 85.5 %all-gather.3.cloned.1.call-done = bf16[2,8192,128]{1,2,0:T(8,128)(2,1)} async-done(((bf16[2,256,128]{1,2,0:T(8,128)(2,1)}), bf16[2,8192,128]{1,2,0:T(8,128)(2,1)}) %all-gather.3.cloned.1.call-update) | async-done | bytes 4194320 | tf_op jit(solution)/shard_map/all_gather | solution.py:78
  384.8 0.0 copy-done.4
  384.8 6.5 %fusion.23 = bf16[2,384,128]{1,2,0:T(8,128)(2,1)S(1)} fusion(bf16[2,8192,128]{1,2,0:T(8,128)(2,1)} %all-gather.3.cloned.1.call-done, bf16[384,8192]{1,0:T(8,128)(2,1)} %all-gather.5.cloned.1.call-done, f32[8192]{0:T(1024)S(1)} %copy-done.4, f32[384]{0:T(512)S(1)} %add_rsqrt_fusion), kind=kOutput, calls=%fused_computation.36 | convolution fusion | flops 1623392256 | bytes 10716672 | tf_op jit(solution)/shard_map/td,jdk->jtk/dot_general | solution.py:75
  391.3 0.8 copy.25
  (2 shorter events, 0.0 us)
Async XLA Ops:
  7.2 82.7 %reduce-scatter.5.cloned.1.call-start = ((), (), s32[]{:S(2)}) async-start(), calls=%async_computation.4 | async-start | bytes 7077888 | tf_op jit(solution)/shard_map/reduce_scatter | solution.py:62
  7.9 208.3 %reduce-scatter.3.cloned.1.call-start = ((), (), s32[]{:S(2)}) async-start(), calls=%async_computation.2 | async-start | bytes 4325376 | tf_op jit(solution)/shard_map/reduce_scatter | solution.py:55
  42.5 9.0 %copy-start.1 = (s32[1,2,256,128]{3,2,1,0:T(8,128)S(1)}, s32[1,2,256,128]{3,2,1,0:T(8,128)}, u32[]{:S(2)}) copy-start(s32[1,2,256,128]{3,2,1,0:T(8,128)} %param.8) | copy-start | bytes 786436
  64.3 25.6 %copy-start = (bf16[384,1024]{1,0:T(8,128)(2,1)S(1)}, bf16[384,1024]{1,0:T(8,128)(2,1)}, u32[]{:S(2)}) copy-start(bf16[384,1024]{1,0:T(8,128)(2,1)} %param.12) | copy-start | bytes 2359300
  64.3 28.0 %copy-start.2 = (f32[2,256,128]{2,1,0:T(8,128)S(1)}, f32[2,256,128]{2,1,0:T(8,128)}, u32[]{:S(2)}) copy-start(f32[2,256,128]{2,1,0:T(8,128)} %param.10) | copy-start | bytes 786436
  64.3 28.1 %copy-start.3 = (f32[2,256,128]{2,1,0:T(8,128)S(1)}, f32[2,256,128]{2,1,0:T(8,128)}, u32[]{:S(2)}) copy-start(f32[2,256,128]{2,1,0:T(8,128)} %param.9) | copy-start | bytes 786436
  85.9 298.9 %copy-start.4 = (f32[8192]{0:T(1024)S(1)}, f32[8192]{0:T(1024)}, u32[]{:S(2)}) copy-start(f32[8192]{0:T(1024)} %param.13) | copy-start | bytes 98308
  85.9 209.3 %all-gather.5.cloned.1.call-start = ((), (), s32[]{:S(2)}) async-start(), calls=%async_computation.5 | async-start | bytes 7077888 | tf_op jit(solution)/shard_map/all_gather | solution.py:69
  92.2 292.6 %all-gather.3.cloned.1.call-start = ((), (), s32[]{:S(2)}) async-start(), calls=%async_computation.3 | async-start | bytes 4325376 | tf_op jit(solution)/shard_map/all_gather | solution.py:78
Sparse Core Ops, SparseCore 0:
  10.6 79.2 reduce-scatter.4
  94.1 122.0 reduce-scatter.2
  218.2 77.0 all-gather.4
  298.6 86.2 all-gather.2
where the time goes:
time: 399 us
  waiting for transfers between devices  289 us (72%)
  local copies, waits for them, and re-layouts  55.8 us (14%)
  other arithmetic  33 us (8%)
  between operations  13.8 us (3%)
  matrix products  6.49 us (2%)
    reduce_scatter x1, waiting for transfers between devices, per_device(): lax.psum_scatter(decoded, 'replica', scatter_dimension=1, tiled=True)  124 us
    all_gather x1, waiting for transfers between devices, per_device(): lax.all_gather(fragment, 'replica', axis=1, tiled=True)  85.5 us
    all_gather x1, waiting for transfers between devices, per_device(): hidden = lax.all_gather(hidden_share, 'tensor', axis=1, tiled=True)  75.7 us
    another operation x1, local copies, waits for them, and re-layouts, unpack_codes(): stacked = jnp.stack(nibbles, axis=2)  31.3 us
    convert_element_type x1, other arithmetic, decode_block(): return shaped.reshape(codes.shape).astype(jnp.bfloat16)  21.6 us
    mul x2, local copies, waits for them, and re-layouts, decode_block(): value.reshape(codes.shape[0], codes.shape[1] // BLOCK, BLOCK, codes.shape...  12.7 us
    reshape x1, local copies, waits for them, and re-layouts, unpack_codes(): return stacked.reshape(words.shape[0], words.shape[1] * 2, words.shape[2])  8.99 us
  transfers between devices with their start and end apart: 4, of which 4 were waited for; matrix products, arithmetic and copies ran while one was open for 22% of the time, Pallas kernels for 0%

commit v1 on v0

v1 whole, which is shorter than its diff:
```python
import jax
import jax.numpy as jnp
from jax import lax
from jax.experimental import pallas as pl
from jax.experimental.pallas import tpu as pltpu
from jax.sharding import PartitionSpec as P

D = 8192
TOK = 384
MESH = pl.DeviceIdType.MESH
F32 = jnp.float32
BF16 = jnp.bfloat16

outer_rate = 0.7
outer_beta = 0.9
norm_epsilon = 1e-05

Y_FIRST = (0, 1, 2, 3, 4)
X_FIRST = (5, 6, 7)
H_ORDER = (0, 5, 1, 2, 6, 3, 4, 7)


class Slots:
    def __init__(self):
        self.total = 0
        self.base = {}

    def add(self, name, count):
        self.base[name] = self.total
        self.total += count

    def __getitem__(self, name):
        return self.base[name]


RECV = Slots()
for _name, _count in (
    ("sib", 4), ("z", 4 * 2 * 4), ("xh", 4), ("a2a", 16), ("ag", 4 * 2 * 2), ("ya", 8 * 2), ("yb", 8 * 2),
    ("yc", 8 * 2), ("xl", 8), ("asib", 8), ("ss", 8), ("p", 16),
):
    RECV.add(_name, _count)
N_SEND = 192
LOCAL = Slots()
for _name, _count in (("codes", 4), ("part", 8), ("misc", 5), ("out", 9)):
    LOCAL.add(_name, _count)


def decode_nibble(code):
    magnitude = jnp.bitwise_and(code, 7).astype(F32)
    value = jnp.maximum(jnp.maximum(0.5 * magnitude, magnitude - 2.0), 2.0 * magnitude - 8.0)
    return jnp.where(code >= 8, -value, value)


def kernel(
    codes, exps, params, momentum, partials, residual, gain,
    kv_out, params_out, momentum_out,
    cbuf, ebuf, pbuf, mbuf, rbuf, gbuf,
    dec, sibr, zrecv, zout, fin, xout, xrecv, grad, newp, newm, frag, wbuf,
    part, yra, yrb, yrc, yout, hs, xo, xr, xr4, xs, abuf, ssacc, ssout, ssr, pout, precv, invb, kvbuf,
    ssem, rsem, lsem,
):
    r = lax.axis_index("replica")
    t = lax.axis_index("tensor")
    xh = r // 16
    z = lax.rem(r // 2, 8)
    c = lax.rem(r, 2)
    xl = t // 4
    y = lax.rem(t, 4)

    def dev(xh_, z_, c_, xl_, y_):
        return (xh_ * 16 + z_ * 2 + c_, xl_ * 4 + y_)

    def zp(n):
        return lax.rem(z + 8 + n, 8)

    def yp(n):
        return lax.rem(y + 4 + n, 4)

    sibling = dev(xh, z, 1 - c, xl, y)
    x_pair = dev(xh, z, c, 1 - xl, y)
    xh_pair = dev(1 - xh, z, c, xl, y)
    z_next = (dev(xh, zp(1), c, xl, y), dev(xh, zp(-1), c, xl, y))
    y_next = (dev(xh, z, c, xl, yp(1)), dev(xh, z, c, xl, yp(-1)))

    sends = []

    def send(src, dst, recv_index, device, cond=None):
        index = len(sends)
        copy = pltpu.make_async_remote_copy(
            src_ref=src, dst_ref=dst, send_sem=ssem.at[index], recv_sem=rsem.at[recv_index],
            device_id=device, device_id_type=MESH,
        )
        if cond is None:
            copy.start()
        else:
            @pl.when(cond)
            def _():
                copy.start()
        sends.append((copy, cond))

    def wait_recv(dst, recv_index):
        pltpu.make_async_remote_copy(
            src_ref=dst, dst_ref=dst, send_sem=ssem.at[0], recv_sem=rsem.at[recv_index],
            device_id=sibling, device_id_type=MESH,
        ).wait_recv()

    def load(src, dst, index):
        copy = pltpu.make_async_copy(src, dst, lsem.at[index])
        copy.start()
        return copy

    code_loads = [None] * 4
    part_loads = [None] * 8

    def load_codes(q):
        code_loads[q] = load(codes.at[q // 2, :, q % 2], cbuf.at[q], LOCAL["codes"] + q)

    def load_part(k):
        part_loads[k] = load(partials.at[:, pl.ds(1024 * k, 1024)], part.at[k], LOCAL["part"] + k)

    exp_load = load(exps, ebuf, LOCAL["misc"])
    load_codes(0)
    res_load = load(residual, rbuf, LOCAL["misc"] + 1)
    load_part(H_ORDER[0])
    load_part(H_ORDER[1])
    load_codes(1)
    load_part(H_ORDER[2])
    load_codes(2)
    load_codes(3)
    for k in H_ORDER[3:]:
        load_part(k)
    param_load = load(params, pbuf, LOCAL["misc"] + 2)
    momentum_load = load(momentum, mbuf, LOCAL["misc"] + 3)
    gain_load = load(gain, gbuf, LOCAL["misc"] + 4)

    barrier = pltpu.get_barrier_semaphore()
    for a in range(2):
        for b in range(2):
            for d in range(2):
                for e in range(4):
                    if a + b + d + e:
                        other = dev(
                            1 - xh if a else xh, z, 1 - c if b else c, 1 - xl if d else xl, yp(e)
                        )
                        pl.semaphore_signal(barrier, inc=1, device_id=other, device_id_type=MESH)
    for other in z_next:
        pl.semaphore_signal(barrier, inc=1, device_id=other, device_id_type=MESH)

    def decode(q, core):
        j, half = q // 2, q % 2

        @pl.loop(0, 16)
        def _(i):
            owner = i * 2 + core
            for b in range(4):
                exponent = ebuf[j, owner, pl.ds(4 * half + b, 1), :]
                scale = jnp.left_shift(jnp.ones_like(exponent), exponent + 5).astype(F32) * 2.0**-5
                words = cbuf[q, owner, pl.ds(16 * b, 16), :]
                low = decode_nibble(jnp.bitwise_and(words, 15)) * scale
                high = decode_nibble(jnp.bitwise_and(jnp.right_shift(words, 4), 15)) * scale
                dec[q, core, i // 8, lax.rem(i, 8), pl.ds(16 * b, 16), :] = low.astype(BF16)
                dec[q, core, i // 8, lax.rem(i, 8), pl.ds(64 + 16 * b, 16), :] = high.astype(BF16)

    tasks = []

    def task(time, function, *arguments):
        tasks.append((time, len(tasks), function, arguments))

    def g_decode_other(q):
        code_loads[q].wait()
        if q == 0:
            exp_load.wait()
        decode(q, 1 - c)
        if q == 0:
            pl.semaphore_wait(barrier, 33)
        send(dec.at[q, 1 - c], sibr.at[q], RECV["sib"] + q, sibling)

    def g_decode_own(q):
        decode(q, c)

    def g_pair(q):
        wait_recv(sibr.at[q], RECV["sib"] + q)

        @pl.loop(0, 16)
        def _(i):
            a, b = i // 8, lax.rem(i, 8)
            dec[q, c, a, b] = (dec[q, c, a, b].astype(F32) + sibr[q, a, b].astype(F32)).astype(BF16)

        for d in range(2):
            send(dec.at[q, c, d, zp(4)], zrecv.at[q, d, 0, d], RECV["z"] + (q * 2 + d) * 4, z_next[d])

    def g_ring(q, step):
        for d in range(2):
            sign = 1 - 2 * d
            target = zp(sign * (5 - step))
            index = RECV["z"] + (q * 2 + d) * 4 + step - 2
            if step == 2:
                wait_recv(zrecv.at[q, d, 0, d], index)
                zout[q, d, step - 2, d] = (
                    dec[q, c, d, target].astype(F32) + zrecv[q, d, 0, d].astype(F32)
                ).astype(BF16)
                zout[q, d, step - 2, 1 - d] = dec[q, c, 1 - d, target]
            else:
                wait_recv(zrecv.at[q, d, step - 2], index)
                for a in range(2):
                    zout[q, d, step - 2, a] = (
                        dec[q, c, a, target].astype(F32) + zrecv[q, d, step - 2, a].astype(F32)
                    ).astype(BF16)
            send(zout.at[q, d, step - 2], zrecv.at[q, d, step - 1], index + 1, z_next[d])

    def g_final(q):
        for d in range(2):
            wait_recv(zrecv.at[q, d, 3], RECV["z"] + (q * 2 + d) * 4 + 3)

        def total(a):
            return (
                dec[q, c, a, z].astype(F32) + zrecv[q, 0, 3, a].astype(F32) + zrecv[q, 1, 3, a].astype(F32)
            )

        xout[q] = total(1 - xh).astype(BF16)
        send(xout.at[q], xrecv.at[q], RECV["xh"] + q, xh_pair)
        fin[q] = total(xh)

    is_source = xl == lax.rem(z, 2)

    def g_update(q):
        j, half = q // 2, q % 2
        if q == 0:
            param_load.wait()
            momentum_load.wait()
        wait_recv(xrecv.at[q], RECV["xh"] + q)
        summed = fin[q] + xrecv[q].astype(F32)
        grad[q, pl.ds(0, 64, stride=2), :] = summed[:64]
        grad[q, pl.ds(1, 64, stride=2), :] = summed[64:]
        outer_grad = grad[q] * (1.0 / 32.0)
        rows = pl.ds(128 * half, 128)
        new_momentum = outer_beta * mbuf[j, rows, :] + outer_grad
        new_params = pbuf[j, rows, :] - outer_rate * (outer_grad + outer_beta * new_momentum)
        newm[j, rows, :] = new_momentum
        newp[j, rows, :] = new_params
        frag[q] = new_params.astype(BF16)
        y_to = 2 * c + half
        x_to = lax.rem(z, 2)
        column = lax.rem(y - y_to + 4 + 3, 4) * 2 + xl
        slot = wbuf.at[(z // 2) * 2 + xh, :, pl.ds(pl.multiple_of(128 * column, 128), 128)]
        index = RECV["a2a"] + xh * 8 + column
        here = (c == j) & (xl == x_to) & (y == y_to)

        @pl.when(here)
        def _():
            pltpu.make_async_copy(frag.at[q], slot, rsem.at[index]).start()

        send(frag.at[q], slot, index, dev(xh, z, j, x_to, y_to), jnp.logical_not(here))
        send(frag.at[q], slot, index, dev(1 - xh, z, j, x_to, y_to))

    def w_block(source_z, i):
        return wbuf.at[pl.ds((source_z // 2) * 2, 2), :, pl.ds(256 * i, 256)]

    def w_half(source_z, a, i):
        return wbuf.at[(source_z // 2) * 2 + a, :, pl.ds(256 * i, 256)]

    def ag_index(i, d, step):
        return RECV["ag"] + (i * 2 + d) * 2 + step

    def w_first(i):
        @pl.when(is_source)
        def _():
            for a in range(2):
                for column in (2 * i, 2 * i + 1):
                    piece = wbuf.at[(z // 2) * 2 + a, :, pl.ds(128 * column, 128)]
                    wait_recv(piece, RECV["a2a"] + a * 8 + column)

        for d in range(2):
            sign = 1 - 2 * d

            @pl.when(jnp.logical_not(is_source))
            def _():
                wait_recv(w_block(zp(-sign), i), ag_index(i, d, 0))

            origin = jnp.where(is_source, z, zp(-sign))
            send(w_block(origin, i), w_block(origin, i), ag_index(i, d, 0), z_next[d])

    def w_second(i):
        for d in range(2):
            sign = 1 - 2 * d

            @pl.when(is_source)
            def _():
                wait_recv(w_block(zp(-2 * sign), i), ag_index(i, d, 0))

            @pl.when(jnp.logical_not(is_source))
            def _():
                wait_recv(w_block(zp(-3 * sign), i), ag_index(i, d, 1))

            block = w_block(zp(-2 * sign), i)
            send(block, block, ag_index(i, d, 1), z_next[d], is_source)
            piece = w_half(zp(-3 * sign), d, i)
            send(piece, piece, ag_index(i, d, 1), z_next[d], jnp.logical_not(is_source))

    def w_last(i):
        @pl.when(is_source)
        def _():
            for d in range(2):
                wait_recv(w_half(zp(4), d, i), ag_index(i, d, 1))

    def lanes(x_, y_):
        return pl.ds(pl.multiple_of(128 * (x_ * 4 + y_), 128), 128)

    def add_rows(out, rows, *terms):
        @pl.loop(0, rows // 64)
        def _(i):
            at = pl.ds(pl.multiple_of(i * 64, 64), 64)
            value = terms[0](at).astype(F32)
            for term in terms[1:]:
                value = value + term(at).astype(F32)
            out(at, value)

    def h_load(k):
        part_loads[k].wait()
        if k == H_ORDER[0]:
            res_load.wait()

        @pl.when(t == k)
        def _():
            @pl.loop(0, TOK // 16)
            def _(i):
                at = pl.ds(pl.multiple_of(i * 16, 16), 16)
                part[k, at, :] = (part[k, at, :].astype(F32) + rbuf[at, :].astype(F32)).astype(BF16)

    def hy_start(k):
        h_load(k)
        n = Y_FIRST.index(k)
        for d in range(2):
            sign = 1 - 2 * d
            send(part.at[k, :, lanes(d, yp(2))], yra.at[n, d], RECV["ya"] + k * 2 + d, y_next[d])
        for d in range(2):
            sign = 1 - 2 * d
            send(part.at[k, :, lanes(1 - d, yp(sign))], yrb.at[n, d], RECV["yb"] + k * 2 + d, y_next[d])

    def hy_middle(k):
        n = Y_FIRST.index(k)
        for d in range(2):
            sign = 1 - 2 * d
            wait_recv(yra.at[n, d], RECV["ya"] + k * 2 + d)
            own = lanes(d, yp(sign))

            def put(at, value, d=d):
                yout[n, d, at, :] = value.astype(BF16)

            add_rows(put, TOK, lambda at, own=own: part[k, at, own], lambda at, d=d: yra[n, d, at, :])
            send(yout.at[n, d], yrc.at[n, d], RECV["yc"] + k * 2 + d, y_next[d])

    def hy_cross(k):
        n = Y_FIRST.index(k)
        for d in range(2):
            wait_recv(yrb.at[n, d], RECV["yb"] + k * 2 + d)
            wait_recv(yrc.at[n, d], RECV["yc"] + k * 2 + d)

        def put_other(at, value):
            xo[n, at, :] = value.astype(BF16)

        def put_own(at, value):
            hs[n, at, :] = value

        for x_, put in ((1 - xl, put_other), (xl, put_own)):
            own = lanes(x_, y)
            add_rows(
                put, TOK, lambda at, own=own: part[k, at, own], lambda at, x_=x_: yrb[n, 1 - x_, at, :],
                lambda at, x_=x_: yrc[n, x_, at, :],
            )
            if put is put_other:
                send(xo.at[n], xr.at[n], RECV["xl"] + k, x_pair)

    first_done = []

    def finish(k, at, value):
        hidden = value.astype(BF16).astype(F32)
        position = (k % 4) * 2 + k // 4
        scaled = hidden * gbuf[pl.ds(8 * k + t, 1), :]
        abuf[c, at, pl.ds(128 * position, 128)] = scaled.astype(BF16)
        if first_done:
            ssacc[at, :] += hidden * hidden
        else:
            ssacc[at, :] = hidden * hidden

    def finished(k):
        first_done.append(k)
        position = (k % 4) * 2 + k // 4
        piece = abuf.at[c, :, pl.ds(128 * position, 128)]
        send(piece, piece, RECV["asib"] + k, sibling)

    def hy_end(k):
        n = Y_FIRST.index(k)
        if not first_done:
            gain_load.wait()
        wait_recv(xr.at[n], RECV["xl"] + k)
        add_rows(
            lambda at, value: finish(k, at, value), TOK, lambda at: hs[n, at, :], lambda at: xr[n, at, :]
        )
        finished(k)

    def hx_start(k):
        h_load(k)
        n = X_FIRST.index(k)
        other = pl.ds(pl.multiple_of(512 * (1 - xl), 512), 512)
        send(part.at[k, :, other], xr4.at[n], RECV["xl"] + k, x_pair)

    half_rows = (pl.ds(0, 192), pl.ds(192, 192))

    def hx_lanes(y_):
        return pl.ds(pl.multiple_of(128 * y_, 128), 128)

    def hx_cross(k):
        n = X_FIRST.index(k)
        wait_recv(xr4.at[n], RECV["xl"] + k)
        own = pl.ds(pl.multiple_of(512 * xl, 512), 512)

        @pl.loop(0, TOK // 16)
        def _(i):
            at = pl.ds(pl.multiple_of(i * 16, 16), 16)
            xs[n, at, :] = (part[k, at, own].astype(F32) + xr4[n, at, :].astype(F32)).astype(BF16)

        for d in range(2):
            send(
                xs.at[n, half_rows[d], hx_lanes(yp(2))], yra.at[len(Y_FIRST) + n, d, pl.ds(0, 192)],
                RECV["ya"] + k * 2 + d, y_next[d],
            )

    def hx_middle(k):
        n = X_FIRST.index(k)
        m = len(Y_FIRST) + n
        for d in range(2):
            sign = 1 - 2 * d
            wait_recv(yra.at[m, d, pl.ds(0, 192)], RECV["ya"] + k * 2 + d)
            own = hx_lanes(yp(sign))

            @pl.loop(0, 192 // 64)
            def _(i, d=d, own=own):
                at = pl.ds(pl.multiple_of(192 * d + i * 64, 64), 64)
                got = pl.ds(pl.multiple_of(i * 64, 64), 64)
                xs[n, at, own] = (xs[n, at, own].astype(F32) + yra[m, d, got, :].astype(F32)).astype(BF16)

            send(xs.at[n, :, own], yrc.at[m, d], RECV["yc"] + k * 2 + d, y_next[d])

    def hx_end(k):
        n = X_FIRST.index(k)
        m = len(Y_FIRST) + n
        if not first_done:
            gain_load.wait()
        for d in range(2):
            wait_recv(yrc.at[m, d], RECV["yc"] + k * 2 + d)
        own = hx_lanes(y)
        add_rows(
            lambda at, value: finish(k, at, value), TOK, lambda at: xs[n, at, own],
            lambda at: yrc[m, 0, at, :], lambda at: yrc[m, 1, at, :],
        )
        finished(k)

    def ss_send():
        for b in range(3):
            block = jnp.sum(ssacc[pl.ds(128 * b, 128), :].T, axis=0, keepdims=True)
            ssout[:, pl.ds(128 * b, 128)] = jnp.broadcast_to(block, (8, 128))
        ssr[t] = ssout[...]
        for d in range(2):
            for e in range(4):
                if d + e:
                    device = dev(xh, z, c, 1 - xl if d else xl, yp(e))
                    send(ssout, ssr.at[t], RECV["ss"] + t, device)

    def ss_receive():
        total = ssr[t]
        for d in range(2):
            for e in range(4):
                if d + e:
                    source = (1 - xl if d else xl) * 4 + yp(e)
                    wait_recv(ssr.at[source], RECV["ss"] + source)
        total = ssr[0]
        for source in range(1, 8):
            total = total + ssr[source]
        inverse = lax.rsqrt(total * (1.0 / D) + norm_epsilon) * D**-0.5
        for b in range(3):
            block = jnp.broadcast_to(inverse[0:1, 128 * b : 128 * b + 128], (128, 128))
            invb[pl.ds(128 * b, 128), :] = block.T

    def project(i):
        if i == 0:
            for k in range(8):
                position = (k % 4) * 2 + k // 4
                wait_recv(abuf.at[1 - c, :, pl.ds(128 * position, 128)], RECV["asib"] + k)
        w = wbuf[:, :, pl.ds(256 * i, 256)].reshape(1024, 256)
        y_to = yp(1 + i)
        for b in range(2):
            pout[i, b] = jnp.dot(abuf[b], w, preferred_element_type=F32).astype(BF16)
            for x_to in range(2):
                piece = pout.at[i, b, :, pl.ds(128 * x_to, 128)]
                slot = precv.at[c, t]
                index = RECV["p"] + c * 8 + t
                device = dev(xh, z, b, x_to, y_to)
                if i < 3:
                    send(piece, slot, index, device)
                else:
                    here = (c == b) & (xl == x_to)

                    @pl.when(here)
                    def _():
                        pltpu.make_async_copy(piece, slot, rsem.at[index]).start()

                    send(piece, slot, index, device, jnp.logical_not(here))

    def result():
        for j in range(2):
            for source in range(8):
                wait_recv(precv.at[j, source], RECV["p"] + j * 8 + source)

            @pl.loop(0, TOK // 32)
            def _(i):
                at = pl.ds(pl.multiple_of(i * 32, 32), 32)
                value = precv[j, 0, at, :].astype(F32)
                for source in range(1, 8):
                    value = value + precv[j, source, at, :].astype(F32)
                kvbuf[j, at, :] = (value * invb[at, :]).astype(BF16)

    starts = (0.0, 1.0, 5.0, 6.0)
    for q in range(4):
        task(0.0 + 1.2 * q, g_decode_other, q)
        task(0.6 + 1.2 * q, g_decode_own, q)
        task(4.5 + starts[q], g_pair, q)
        for step in (2, 3, 4):
            task(4.5 + starts[q] + 4.0 * (step - 1), g_ring, q, step)
        task(20.5 + starts[q], g_final, q)
        task(24.5 + starts[q], g_update, q)
    for i in range(4):
        task(36.0 + 2.0 * i, w_first, i)
        task(44.0 + 3.0 * i, w_second, i)
        task(55.0 + 3.0 * i, w_last, i)
        task(55.1 + 3.0 * i, project, i)
    for n, k in enumerate(H_ORDER):
        start = 0.3 + 1.5 * n if n < 3 else 4.0 + 5.0 * (n - 2)
        if k in Y_FIRST:
            task(start, hy_start, k)
            task(start + 7.0, hy_middle, k)
            task(start + 14.0, hy_cross, k)
            task(start + 19.0, hy_end, k)
        else:
            task(start, hx_start, k)
            task(start + 10.0, hx_cross, k)
            task(start + 15.0, hx_middle, k)
            task(start + 20.0, hx_end, k)
    task(52.0, ss_send)
    task(64.3, ss_receive)
    task(70.0, result)
    outs = []
    for _, _, function, arguments in sorted(tasks, key=lambda item: item[:2]):
        function(*arguments)
        if function is g_update and arguments == (3,):
            outs.append(load(newp, params_out, LOCAL["out"]))
            outs.append(load(newm, momentum_out, LOCAL["out"] + 1))
    outs.append(load(kvbuf, kv_out, LOCAL["out"] + 2))
    for copy, cond in sends:
        if cond is None:
            copy.wait_send()
        else:
            @pl.when(cond)
            def _():
                copy.wait_send()
    for copy in outs:
        copy.wait()


def per_device(
    delta_codes, scale_exponents, outer_params, outer_momentum, tensor_partials, residual_stream, norm_gain
):
    ny, nx = len(Y_FIRST), len(X_FIRST)
    vmem = pltpu.VMEM
    scratch = [
        vmem((4, 32, 64, 128), jnp.int32),
        vmem((2, 32, 8, 128), jnp.int32),
        vmem((2, 256, 128), F32),
        vmem((2, 256, 128), F32),
        vmem((TOK, 1024), BF16),
        vmem((64, 128), F32),
        vmem((4, 2, 2, 8, 128, 128), BF16),
        vmem((4, 2, 8, 128, 128), BF16),
        vmem((4, 2, 4, 2, 128, 128), BF16),
        vmem((4, 2, 3, 2, 128, 128), BF16),
        vmem((4, 128, 128), F32),
        vmem((4, 128, 128), BF16),
        vmem((4, 128, 128), BF16),
        vmem((4, 128, 128), F32),
        vmem((2, 256, 128), F32),
        vmem((2, 256, 128), F32),
        vmem((4, 128, 128), BF16),
        vmem((8, 128, 1024), BF16),
        vmem((8, TOK, 1024), BF16),
        vmem((8, 2, TOK, 128), BF16),
        vmem((ny, 2, TOK, 128), BF16),
        vmem((8, 2, TOK, 128), BF16),
        vmem((ny, 2, TOK, 128), BF16),
        vmem((ny, TOK, 128), F32),
        vmem((ny, TOK, 128), BF16),
        vmem((ny, TOK, 128), BF16),
        vmem((nx, TOK, 512), BF16),
        vmem((nx, TOK, 512), BF16),
        vmem((2, TOK, 1024), BF16),
        vmem((TOK, 128), F32),
        vmem((8, TOK), F32),
        vmem((8, 8, TOK), F32),
        vmem((4, 2, TOK, 256), BF16),
        vmem((2, 8, TOK, 128), BF16),
        vmem((TOK, 128), F32),
        vmem((2, TOK, 128), BF16),
        pltpu.SemaphoreType.DMA((N_SEND,)),
        pltpu.SemaphoreType.DMA((RECV.total,)),
        pltpu.SemaphoreType.DMA((LOCAL.total,)),
    ]
    any_spec = pl.BlockSpec(memory_space=pl.ANY)
    return pl.pallas_call(
        kernel,
        out_shape=(
            jax.ShapeDtypeStruct((2, TOK, 128), BF16),
            jax.ShapeDtypeStruct((2, 256, 128), F32),
            jax.ShapeDtypeStruct((2, 256, 128), F32),
        ),
        in_specs=[any_spec] * 7,
        out_specs=(any_spec,) * 3,
        scratch_shapes=scratch,
        compiler_params=pltpu.CompilerParams(
            collective_id=0, has_side_effects=True, vmem_limit_bytes=60 * 2**20
        ),
        cost_estimate=pl.CostEstimate(flops=2 * 768 * 1024 * 1024, bytes_accessed=13 * 2**20, transcendentals=0),
        name="outer_step",
    )(
        delta_codes.reshape(2, 32, 2, 64, 128),
        scale_exponents.reshape(2, 32, 8, 128),
        outer_params,
        outer_momentum,
        tensor_partials.reshape(TOK, D),
        residual_stream,
        norm_gain.reshape(64, 128),
    )


def solution(mesh):
    return jax.shard_map(
        per_device,
        mesh=mesh,
        in_specs=(
            P("replica", None, None, "tensor"),
            P("replica", None, None, "tensor"),
            P(None, "replica", "tensor"),
            P(None, "replica", "tensor"),
            P("tensor", "replica", None),
            P("replica", "tensor"),
            P(),
        ),
        out_specs=(
            P(None, "replica", "tensor"),
            P(None, "replica", "tensor"),
            P(None, "replica", "tensor"),
        ),
        check_vma=False,
    )
```

time: 399 us -> 116 us (0.29)
  the two profiles are of different devices: /device:TPU:1 before, /device:TPU:25 now
where the time goes in v1:
time: 116 us
  Pallas kernels  110 us (95%)
  local copies, waits for them, and re-layouts  4.96 us (4%)
    pallas_call x1, Pallas kernels, per_device(): pl.pallas_call(kernel, out_shape=(jax.ShapeDtypeStruct((2, TOK, 128), BF1...  110 us
    unnamed x3, local copies, waits for them, and re-layouts  4.96 us

profile of v1, /device:TPU:25, one launch (start us, length us, event | category | flops | bytes accessed | tf_op | source)
XLA Modules:
  0.0 115.7 jit_solution(12531537562811838016)
XLA Ops:
  0.6 110.1 %outer_step.1 = (bf16[2,384,128]{2,1,0:T(8,128)(2,1)}, f32[2,256,128]{2,1,0:T(8,128)}, f32[2,256,128]{2,1,0:T(8,128)}) custom-call(s32[2,32,2,64,128]{4,3,2,1,0:T(8,128)} %bitcast.5, s32[2,32,8,128]{3,2,1,0:T(8,128)} %bitcast.6, f32[2,256,128]{2,1,0:T(8,128)} %params.1, f32[2,256,128]{2,1,0:T(8,128)} %momentum.1, bf16[384,8192]{1,0:T(8,128)(2,1)} %bitcast.4, ...), custom_call_target="tpu_custom_call" | custom-call | flops 1610612736 | bytes 13631488 | tf_op jit(solution)/shard_map/outer_step/pallas_call | solution.py:617
  110.8 1.6 %copy.13 = bf16[2,384,128]{2,1,0:T(8,128)(2,1)} copy(bf16[2,384,128]{2,1,0:T(8,128)(2,1)} %get-tuple-element.6) | data formatting | bytes 393216
  112.4 1.7 %copy.14 = f32[2,256,128]{2,1,0:T(8,128)} copy(f32[2,256,128]{2,1,0:T(8,128)} %get-tuple-element.7) | data formatting | bytes 524288
  114.1 1.7 %copy.15 = f32[2,256,128]{2,1,0:T(8,128)} copy(f32[2,256,128]{2,1,0:T(8,128)} %get-tuple-element.8) | data formatting | bytes 524288

commit v2 on v1

v2 whole, which is shorter than its diff:
```python
import jax
import jax.numpy as jnp
from jax import lax
from jax.experimental import pallas as pl
from jax.experimental.pallas import tpu as pltpu
from jax.sharding import PartitionSpec as P

D = 8192
TOK = 384
MESH = pl.DeviceIdType.MESH
F32 = jnp.float32
BF16 = jnp.bfloat16

outer_rate = 0.7
outer_beta = 0.9
norm_epsilon = 1e-05

Y_FIRST = (0, 1, 2, 3, 4, 5, 6)
X_FIRST = (7,)
H_ORDER = (0, 7, 1, 2, 3, 4, 5, 6)


PLAN = {
    "other": (1.5, 3.7, 6.8, 10.0),
    "own": (3.0, 5.4, 7.5, 10.7),
    "pair": (4.9, 6.3, 9.6, 13.0),
    "hop": 3.5,
    "cross": 4.0,
    "gather": (29.0, 37.0),
    "piece": 0.8,
    "relay": 4.0,
    "start": (3.1, 3.2, 5.5, 10.5, 15.0, 19.0, 24.0, 29.0),
    "y": (0.0, 7.0, 14.0, 19.0),
    "x": (0.0, 10.0, 15.0, 20.0, 24.0),
    "greet": (6.0, 9.0, 12.0, 14.0),
    "squares": 8.0,
}


class Slots:
    def __init__(self):
        self.total = 0
        self.base = {}

    def add(self, name, count):
        self.base[name] = self.total
        self.total += count

    def __getitem__(self, name):
        return self.base[name]


RECV = Slots()
for _name, _count in (
    ("sib", 4), ("z", 4 * 2 * 4), ("xh", 4), ("a2a", 8), ("ag", 4 * 2 * 4), ("ya", 8 * 2), ("yb", 8 * 2),
    ("yc", 8 * 2), ("xl", 8 * 2), ("asib", 8 * 2), ("ss", 4), ("p", 8),
):
    RECV.add(_name, _count)
N_SEND = 256
LOCAL = Slots()
for _name, _count in (("codes", 4), ("part", 8), ("misc", 5), ("out", 9)):
    LOCAL.add(_name, _count)


def decode_nibble(code):
    magnitude = jnp.bitwise_and(code, 7).astype(F32)
    value = jnp.maximum(jnp.maximum(0.5 * magnitude, magnitude - 2.0), 2.0 * magnitude - 8.0)
    return jnp.where(code >= 8, -value, value)


def kernel(
    codes, exps, params, momentum, partials, residual, gain,
    kv_out, params_out, momentum_out,
    cbuf, ebuf, pbuf, mbuf, rbuf, gbuf,
    dec, sibr, zrecv, zout, fin, xout, xrecv, grad, newp, newm, frag, wbuf,
    part, yra, yrb, yrc, yout, xo, xr, xr4, xs, abuf, ssacc, ssout, ssr, pout, precv, invb, kvbuf,
    ssem, rsem, lsem, plane,
):
    r = lax.axis_index("replica")
    t = lax.axis_index("tensor")
    xh = r // 16
    z = lax.rem(r // 2, 8)
    c = lax.rem(r, 2)
    xl = t // 4
    y = lax.rem(t, 4)

    def dev(xh_, z_, c_, xl_, y_):
        return (xh_ * 16 + z_ * 2 + c_, xl_ * 4 + y_)

    def zp(n):
        return lax.rem(z + 8 + n, 8)

    def yp(n):
        return lax.rem(y + 4 + n, 4)

    sibling = dev(xh, z, 1 - c, xl, y)
    x_pair = dev(xh, z, c, 1 - xl, y)
    x_cross = dev(1 - xh, z, c, 1 - xl, y)
    xh_pair = dev(1 - xh, z, c, xl, y)
    z_next = (dev(xh, zp(1), c, xl, y), dev(xh, zp(-1), c, xl, y))
    y_next = (dev(xh, z, c, xl, yp(1)), dev(xh, z, c, xl, yp(-1)))

    sends = []

    def send(src, dst, recv_index, device, cond=None, inside=None, like=None):
        index = len(sends)
        copy = pltpu.make_async_remote_copy(
            src_ref=src, dst_ref=dst, send_sem=ssem.at[index], recv_sem=rsem.at[recv_index],
            device_id=device, device_id_type=MESH,
        )
        if cond is None:
            copy.start()
        else:
            pl.when(cond)(copy.start)
        sends.append((src if like is None else like, cond if inside is None else inside))

    def wait_send(index):
        like, cond = sends[index]
        copy = pltpu.make_async_remote_copy(
            src_ref=like, dst_ref=like, send_sem=ssem.at[index], recv_sem=rsem.at[0],
            device_id=sibling, device_id_type=MESH,
        )
        if cond is None:
            copy.wait_send()
        else:
            pl.when(cond)(copy.wait_send)

    def wait_recv(dst, recv_index):
        pltpu.make_async_remote_copy(
            src_ref=dst, dst_ref=dst, send_sem=ssem.at[0], recv_sem=rsem.at[recv_index],
            device_id=sibling, device_id_type=MESH,
        ).wait_recv()

    def load(src, dst, index):
        copy = pltpu.make_async_copy(src, dst, lsem.at[index])
        copy.start()
        return copy

    code_loads = [None] * 4
    part_loads = [None] * 8

    def load_codes(q):
        code_loads[q] = load(codes.at[q // 2, :, q % 2], cbuf.at[q], LOCAL["codes"] + q)

    def load_part(k):
        part_loads[k] = load(partials.at[:, pl.ds(1024 * k, 1024)], part.at[k], LOCAL["part"] + k)

    load_codes(0)
    exp_load = load(exps, ebuf, LOCAL["misc"])
    res_load = load(residual, rbuf, LOCAL["misc"] + 1)
    load_part(H_ORDER[0])
    state_loads = []

    def more_loads():
        load_part(H_ORDER[1])
        load_codes(1)
        load_part(H_ORDER[2])
        load_codes(2)
        load_codes(3)
        for k in H_ORDER[3:]:
            load_part(k)
        state_loads.append(load(gain, gbuf, LOCAL["misc"] + 4))
        state_loads.append(load(params, pbuf, LOCAL["misc"] + 2))
        state_loads.append(load(momentum, mbuf, LOCAL["misc"] + 3))

    barrier = pltpu.get_barrier_semaphore()
    for other in (sibling, x_pair, x_cross) + y_next + z_next:
        pl.semaphore_signal(barrier, inc=1, device_id=other, device_id_type=MESH)

    def greet(stage):
        others = (y_next, (x_pair, x_cross), (x_pair, x_cross), (sibling,))
        if stage:
            pl.semaphore_wait(plane.at[stage - 1], len(others[stage - 1]))
        if stage < 4:
            for other in others[stage]:
                pl.semaphore_signal(plane.at[stage], inc=1, device_id=other, device_id_type=MESH)

    def decode(q, core):
        j, half = q // 2, q % 2

        @pl.loop(0, 16)
        def _(i):
            owner = i * 2 + core
            for b in range(4):
                exponent = ebuf[j, owner, pl.ds(4 * half + b, 1), :]
                scale = jnp.left_shift(jnp.ones_like(exponent), exponent + 5).astype(F32) * 2.0**-5
                words = cbuf[q, owner, pl.ds(16 * b, 16), :]
                low = decode_nibble(jnp.bitwise_and(words, 15)) * scale
                high = decode_nibble(jnp.bitwise_and(jnp.right_shift(words, 4), 15)) * scale
                dec[q, core, i // 8, lax.rem(i, 8), pl.ds(16 * b, 16), :] = low.astype(BF16)
                dec[q, core, i // 8, lax.rem(i, 8), pl.ds(64 + 16 * b, 16), :] = high.astype(BF16)

    tasks = []

    def task(time, function, *arguments):
        tasks.append((time, len(tasks), function, arguments))

    def g_decode_other(q):
        code_loads[q].wait()
        if q == 0:
            exp_load.wait()
        decode(q, 1 - c)
        if q == 0:
            pl.semaphore_wait(barrier, 7)
            greet(0)
            more_loads()
        send(dec.at[q, 1 - c], sibr.at[q], RECV["sib"] + q, sibling)

    def g_decode_own(q):
        decode(q, c)

    def g_pair(q):
        wait_recv(sibr.at[q], RECV["sib"] + q)

        @pl.loop(0, 16)
        def _(i):
            a, b = i // 8, lax.rem(i, 8)
            dec[q, c, a, b] = (dec[q, c, a, b].astype(F32) + sibr[q, a, b].astype(F32)).astype(BF16)

        for d in range(2):
            send(dec.at[q, c, d, zp(4)], zrecv.at[q, d, 0, d], RECV["z"] + (q * 2 + d) * 4, z_next[d])

    def g_ring(q, step):
        for d in range(2):
            sign = 1 - 2 * d
            target = zp(sign * (5 - step))
            index = RECV["z"] + (q * 2 + d) * 4 + step - 2
            if step == 2:
                wait_recv(zrecv.at[q, d, 0, d], index)
                zout[q, d, step - 2, d] = (
                    dec[q, c, d, target].astype(F32) + zrecv[q, d, 0, d].astype(F32)
                ).astype(BF16)
                zout[q, d, step - 2, 1 - d] = dec[q, c, 1 - d, target]
            else:
                wait_recv(zrecv.at[q, d, step - 2], index)
                for a in range(2):
                    zout[q, d, step - 2, a] = (
                        dec[q, c, a, target].astype(F32) + zrecv[q, d, step - 2, a].astype(F32)
                    ).astype(BF16)
            send(zout.at[q, d, step - 2], zrecv.at[q, d, step - 1], index + 1, z_next[d])

    def g_final(q):
        for d in range(2):
            wait_recv(zrecv.at[q, d, 3], RECV["z"] + (q * 2 + d) * 4 + 3)

        def total(a):
            return (
                dec[q, c, a, z].astype(F32) + zrecv[q, 0, 3, a].astype(F32) + zrecv[q, 1, 3, a].astype(F32)
            )

        xout[q] = total(1 - xh).astype(BF16)
        send(xout.at[q], xrecv.at[q], RECV["xh"] + q, xh_pair)
        fin[q] = total(xh)

    away = (2, 1, 3, 0)

    def place_of(delta):
        return jnp.where(delta == 2, 0, jnp.where(delta == 1, 1, jnp.where(delta == 3, 2, 3)))

    def g_update(q):
        j, half = q // 2, q % 2
        if q == 0:
            state_loads[1].wait()
            state_loads[2].wait()
        wait_recv(xrecv.at[q], RECV["xh"] + q)
        summed = fin[q] + xrecv[q].astype(F32)
        grad[q, pl.ds(0, 64, stride=2), :] = summed[:64]
        grad[q, pl.ds(1, 64, stride=2), :] = summed[64:]
        outer_grad = grad[q] * (1.0 / 32.0)
        rows = pl.ds(128 * half, 128)
        new_momentum = outer_beta * mbuf[j, rows, :] + outer_grad
        new_params = pbuf[j, rows, :] - outer_rate * (outer_grad + outer_beta * new_momentum)
        newm[j, rows, :] = new_momentum
        newp[j, rows, :] = new_params
        frag[q] = new_params.astype(BF16)
        y_to = 2 * c + half
        column = place_of(lax.rem(y - y_to + 4, 4))
        slot = wbuf.at[z * 2 + xh, :, pl.ds(pl.multiple_of(128 * column, 128), 128)]
        index = RECV["a2a"] + xh * 4 + column
        here = (c == j) & (y == y_to)

        @pl.when(here)
        def _():
            pltpu.make_async_copy(frag.at[q], slot, rsem.at[index]).start()

        send(frag.at[q], slot, index, dev(xh, z, j, xl, y_to), jnp.logical_not(here))
        send(frag.at[q], slot, index, dev(1 - xh, z, j, xl, y_to))

    def w_block(source_z, i):
        return wbuf.at[pl.ds(source_z * 2, 2), :, pl.ds(128 * i, 128)]

    def w_half(source_z, a, i):
        return wbuf.at[source_z * 2 + a, :, pl.ds(128 * i, 128)]

    def w_step(i, core, step):
        like = w_block(0, i) if step < 3 else w_half(0, 0, i)
        mine = c == core

        @pl.when(mine)
        def _():
            if step == 0:
                for a in range(2):
                    wait_recv(w_half(z, a, i), RECV["a2a"] + a * 4 + i)
            for d in range(2):
                index = RECV["ag"] + (i * 2 + d) * 4 + step
                origin = zp((2 * d - 1) * step)
                if 0 < step < 4:
                    wait_recv(w_block(origin, i), index - 1)
                if step < 3:
                    send(w_block(origin, i), w_block(origin, i), index, z_next[d], inside=mine, like=like)
                elif step == 3:
                    piece = w_half(origin, d, i)
                    send(piece, piece, index, z_next[d], inside=mine, like=like)
                else:
                    wait_recv(w_half(origin, d, i), index - 1)

    def lanes(x_, y_):
        return pl.ds(pl.multiple_of(128 * (x_ * 4 + y_), 128), 128)

    def add_rows(out, rows, *terms):
        @pl.loop(0, rows // 64)
        def _(i):
            at = pl.ds(pl.multiple_of(i * 64, 64), 64)
            value = terms[0](at).astype(F32)
            for term in terms[1:]:
                value = value + term(at).astype(F32)
            out(at, value)

    def h_load(k):
        part_loads[k].wait()
        if k == H_ORDER[0]:
            res_load.wait()

        @pl.when(t == k)
        def _():
            @pl.loop(0, TOK // 16)
            def _(i):
                at = pl.ds(pl.multiple_of(i * 16, 16), 16)
                part[k, at, :] = (part[k, at, :].astype(F32) + rbuf[at, :].astype(F32)).astype(BF16)

    def hy_start(k):
        h_load(k)
        n = Y_FIRST.index(k)
        for d in range(2):
            sign = 1 - 2 * d
            send(part.at[k, :, lanes(d, yp(2))], yra.at[n, d], RECV["ya"] + k * 2 + d, y_next[d])
        for d in range(2):
            sign = 1 - 2 * d
            send(part.at[k, :, lanes(1 - d, yp(sign))], yrb.at[n, d], RECV["yb"] + k * 2 + d, y_next[d])

    def hy_middle(k):
        n = Y_FIRST.index(k)
        for d in range(2):
            sign = 1 - 2 * d
            wait_recv(yra.at[n, d], RECV["ya"] + k * 2 + d)
            own = lanes(d, yp(sign))

            def put(at, value, d=d):
                yout[n, d, at, :] = value.astype(BF16)

            add_rows(put, TOK, lambda at, own=own: part[k, at, own], lambda at, d=d: yra[n, d, at, :])
            send(yout.at[n, d], yrc.at[n, d], RECV["yc"] + k * 2 + d, y_next[d])

    def hy_cross(k):
        n = Y_FIRST.index(k)
        for d in range(2):
            wait_recv(yrb.at[n, d], RECV["yb"] + k * 2 + d)
            wait_recv(yrc.at[n, d], RECV["yc"] + k * 2 + d)

        for x_ in range(2):
            own = lanes(x_, y)

            def put(at, value, x_=x_):
                xo[n, x_, at, :] = value.astype(BF16)

            add_rows(
                put, TOK, lambda at, own=own: part[k, at, own], lambda at, x_=x_: yrb[n, 1 - x_, at, :],
                lambda at, x_=x_: yrc[n, x_, at, :],
            )
            send(xo.at[n, x_], xr.at[n, x_], RECV["xl"] + k * 2 + x_, x_pair)

    def place_at(k, x_):
        return pl.ds(pl.multiple_of(128 * (((2 * k) % 8) * 2 + 2 * x_ + k // 4), 128), 128)

    def finish(k, x_, at, value):
        hidden = value.astype(BF16).astype(F32)
        scaled = hidden * gbuf[pl.ds(8 * k + 4 * x_ + y, 1), :]
        abuf[c, at, place_at(k, x_)] = scaled.astype(BF16)
        ssacc[at, :] += hidden * hidden

    def finished(k, x_):
        piece = abuf.at[c, :, place_at(k, x_)]
        send(piece, piece, RECV["asib"] + k * 2 + x_, sibling)

    gain_waited = []

    def gain_ready():
        if not gain_waited:
            state_loads[0].wait()
            ssacc[...] = jnp.zeros_like(ssacc)
            gain_waited.append(True)

    def hy_end(k):
        n = Y_FIRST.index(k)
        gain_ready()
        for x_ in range(2):
            wait_recv(xr.at[n, x_], RECV["xl"] + k * 2 + x_)
            add_rows(
                lambda at, value, x_=x_: finish(k, x_, at, value), TOK,
                lambda at, x_=x_: xo[n, x_, at, :], lambda at, x_=x_: xr[n, x_, at, :],
            )
            finished(k, x_)

    def hx_start(k):
        h_load(k)
        n = X_FIRST.index(k)
        other = pl.ds(pl.multiple_of(512 * (1 - xl), 512), 512)
        send(part.at[k, :, other], xr4.at[n], RECV["xl"] + k * 2, x_pair)

    half_rows = (pl.ds(0, 192), pl.ds(192, 192))

    def hx_lanes(y_):
        return pl.ds(pl.multiple_of(128 * y_, 128), 128)

    def hx_cross(k):
        n = X_FIRST.index(k)
        wait_recv(xr4.at[n], RECV["xl"] + k * 2)
        own = pl.ds(pl.multiple_of(512 * xl, 512), 512)

        @pl.loop(0, TOK // 16)
        def _(i):
            at = pl.ds(pl.multiple_of(i * 16, 16), 16)
            xs[n, at, :] = (part[k, at, own].astype(F32) + xr4[n, at, :].astype(F32)).astype(BF16)

        for d in range(2):
            send(
                xs.at[n, half_rows[d], hx_lanes(yp(2))], yra.at[len(Y_FIRST) + n, d, pl.ds(0, 192)],
                RECV["ya"] + k * 2 + d, y_next[d],
            )

    def hx_middle(k):
        n = X_FIRST.index(k)
        m = len(Y_FIRST) + n
        for d in range(2):
            sign = 1 - 2 * d
            wait_recv(yra.at[m, d, pl.ds(0, 192)], RECV["ya"] + k * 2 + d)
            own = hx_lanes(yp(sign))

            @pl.loop(0, 192 // 64)
            def _(i, d=d, own=own):
                at = pl.ds(pl.multiple_of(192 * d + i * 64, 64), 64)
                got = pl.ds(pl.multiple_of(i * 64, 64), 64)
                xs[n, at, own] = (xs[n, at, own].astype(F32) + yra[m, d, got, :].astype(F32)).astype(BF16)

            send(xs.at[n, :, own], yrc.at[m, d], RECV["yc"] + k * 2 + d, y_next[d])

    def hx_end(k):
        n = X_FIRST.index(k)
        m = len(Y_FIRST) + n
        gain_ready()
        for d in range(2):
            wait_recv(yrc.at[m, d], RECV["yc"] + k * 2 + d)
        own = hx_lanes(y)

        def put(at, value):
            xo[m, 0, at, :] = value.astype(BF16)
            finish(k, xl, at, value)

        add_rows(
            put, TOK, lambda at: xs[n, at, own], lambda at: yrc[m, 0, at, :], lambda at: yrc[m, 1, at, :]
        )
        send(xo.at[m, 0], xr.at[m, 0], RECV["xl"] + k * 2 + 1, x_pair)
        finished(k, xl)

    def hx_last(k):
        m = len(Y_FIRST) + X_FIRST.index(k)
        wait_recv(xr.at[m, 0], RECV["xl"] + k * 2 + 1)
        add_rows(lambda at, value: finish(k, 1 - xl, at, value), TOK, lambda at: xr[m, 0, at, :])
        finished(k, 1 - xl)

    def ss_send():
        for b in range(3):
            block = jnp.sum(ssacc[pl.ds(128 * b, 128), :].T, axis=0, keepdims=True)
            ssout[:, pl.ds(128 * b, 128)] = jnp.broadcast_to(block, (8, 128))
        ssr[y] = ssout[...]
        for e in range(1, 4):
            send(ssout, ssr.at[y], RECV["ss"] + y, dev(xh, z, c, xl, yp(e)))

    def ss_receive():
        for e in range(1, 4):
            wait_recv(ssr.at[yp(e)], RECV["ss"] + yp(e))
        total = ssr[0] + ssr[1] + ssr[2] + ssr[3]
        inverse = lax.rsqrt(total * (1.0 / D) + norm_epsilon) * D**-0.5
        for b in range(3):
            block = jnp.broadcast_to(inverse[0:1, 128 * b : 128 * b + 128], (128, 128))
            invb[pl.ds(128 * b, 128), :] = block.T

    def hidden_ready():
        for k in range(8):
            for x_ in range(2):
                wait_recv(abuf.at[1 - c, :, place_at(k, x_)], RECV["asib"] + k * 2 + x_)

    pout_like = pout.at[0, 0]

    def project(i, core):
        mine = c == core

        @pl.when(mine)
        def _():
            w = wbuf[:, :, pl.ds(128 * i, 128)].reshape(2048, 128)
            for b in range(2):
                pout[i, b] = jnp.dot(abuf[b], w, preferred_element_type=F32).astype(BF16)
                slot = precv.at[core, y]
                index = RECV["p"] + core * 4 + y
                if away[i] == 0 and b == core:
                    pltpu.make_async_copy(pout.at[i, b], slot, rsem.at[index]).start()
                else:
                    device = dev(xh, z, b, xl, yp(away[i]))
                    send(pout.at[i, b], slot, index, device, inside=mine, like=pout_like)

    def result():
        for j in range(2):
            for source in range(4):
                wait_recv(precv.at[j, source], RECV["p"] + j * 4 + source)

            @pl.loop(0, TOK // 32)
            def _(i):
                at = pl.ds(pl.multiple_of(i * 32, 32), 32)
                value = precv[j, 0, at, :].astype(F32)
                for source in range(1, 4):
                    value = value + precv[j, source, at, :].astype(F32)
                kvbuf[j, at, :] = (value * invb[at, :]).astype(BF16)

    for q in range(4):
        task(PLAN["other"][q], g_decode_other, q)
        task(PLAN["own"][q], g_decode_own, q)
        base = PLAN["pair"][q]
        task(base, g_pair, q)
        for step in (2, 3, 4):
            task(base + PLAN["hop"] * (step - 1), g_ring, q, step)
        task(base + PLAN["hop"] * 4, g_final, q)
        task(base + PLAN["hop"] * 4 + PLAN["cross"], g_update, q)
    for n, k in enumerate(H_ORDER):
        start = PLAN["start"][n]
        if k in Y_FIRST:
            for function, after in zip((hy_start, hy_middle, hy_cross, hy_end), PLAN["y"]):
                task(start + after, function, k)
        else:
            for function, after in zip((hx_start, hx_cross, hx_middle, hx_end, hx_last), PLAN["x"]):
                task(start + after, function, k)
    hidden_time = max(item[0] for item in tasks if item[2] in (hy_end, hx_last))
    task(hidden_time + 0.01, ss_send)
    task(hidden_time + 0.02, hidden_ready)
    task(hidden_time + PLAN["squares"], ss_receive)
    for core in range(2):
        for i in range(4):
            base = PLAN["gather"][core] + PLAN["piece"] * i
            for step in range(5):
                task(base + PLAN["relay"] * step, w_step, i, core, step)
            task(max(base + PLAN["relay"] * 4, hidden_time) + 0.1, project, i, core)
    for stage, time in zip((1, 2, 3, 4), PLAN["greet"]):
        task(time, greet, stage)
    task(1000.0, result)
    outs = []
    for _, _, function, arguments in sorted(tasks, key=lambda item: item[:2]):
        function(*arguments)
        if function is g_update and arguments == (3,):
            outs.append(load(newp, params_out, LOCAL["out"]))
            outs.append(load(newm, momentum_out, LOCAL["out"] + 1))
    outs.append(load(kvbuf, kv_out, LOCAL["out"] + 2))
    for index in range(len(sends)):
        wait_send(index)
    for copy in outs:
        copy.wait()


def hand_over(*refs):
    ins, outs, held, sems = refs[:3], refs[3:6], refs[6:9], refs[9]
    loads = [pltpu.make_async_copy(ins[n], held[n], sems.at[n]) for n in range(3)]
    stores = [pltpu.make_async_copy(held[n], outs[n], sems.at[3 + n]) for n in range(3)]
    for copy in loads:
        copy.start()
    for load, store in zip(loads, stores):
        load.wait()
        store.start()
    for copy in stores:
        copy.wait()


def per_device(
    delta_codes, scale_exponents, outer_params, outer_momentum, tensor_partials, residual_stream, norm_gain
):
    ny, nx = len(Y_FIRST), len(X_FIRST)
    vmem = pltpu.VMEM
    scratch = [
        vmem((4, 32, 64, 128), jnp.int32),
        vmem((2, 32, 8, 128), jnp.int32),
        vmem((2, 256, 128), F32),
        vmem((2, 256, 128), F32),
        vmem((TOK, 1024), BF16),
        vmem((64, 128), F32),
        vmem((4, 2, 2, 8, 128, 128), BF16),
        vmem((4, 2, 8, 128, 128), BF16),
        vmem((4, 2, 4, 2, 128, 128), BF16),
        vmem((4, 2, 3, 2, 128, 128), BF16),
        vmem((4, 128, 128), F32),
        vmem((4, 128, 128), BF16),
        vmem((4, 128, 128), BF16),
        vmem((4, 128, 128), F32),
        vmem((2, 256, 128), F32),
        vmem((2, 256, 128), F32),
        vmem((4, 128, 128), BF16),
        vmem((16, 128, 512), BF16),
        vmem((8, TOK, 1024), BF16),
        vmem((8, 2, TOK, 128), BF16),
        vmem((ny, 2, TOK, 128), BF16),
        vmem((8, 2, TOK, 128), BF16),
        vmem((ny, 2, TOK, 128), BF16),
        vmem((8, 2, TOK, 128), BF16),
        vmem((8, 2, TOK, 128), BF16),
        vmem((nx, TOK, 512), BF16),
        vmem((nx, TOK, 512), BF16),
        vmem((2, TOK, 2048), BF16),
        vmem((TOK, 128), F32),
        vmem((8, TOK), F32),
        vmem((4, 8, TOK), F32),
        vmem((4, 2, TOK, 128), BF16),
        vmem((2, 4, TOK, 128), BF16),
        vmem((TOK, 128), F32),
        vmem((2, TOK, 128), BF16),
        pltpu.SemaphoreType.DMA((N_SEND,)),
        pltpu.SemaphoreType.DMA((RECV.total,)),
        pltpu.SemaphoreType.DMA((LOCAL.total,)),
        pltpu.SemaphoreType.REGULAR((4,)),
    ]
    any_spec = pl.BlockSpec(memory_space=pl.ANY)
    out_shape = (
        jax.ShapeDtypeStruct((2, TOK, 128), BF16),
        jax.ShapeDtypeStruct((2, 256, 128), F32),
        jax.ShapeDtypeStruct((2, 256, 128), F32),
    )
    outs = pl.pallas_call(
        kernel,
        out_shape=out_shape,
        in_specs=[any_spec] * 7,
        out_specs=(any_spec,) * 3,
        scratch_shapes=scratch,
        compiler_params=pltpu.CompilerParams(
            collective_id=0, has_side_effects=True, vmem_limit_bytes=60 * 2**20
        ),
        cost_estimate=pl.CostEstimate(flops=2 * 768 * 1024 * 1024, bytes_accessed=13 * 2**20, transcendentals=0),
        name="outer_step",
    )(
        delta_codes.reshape(2, 32, 2, 64, 128),
        scale_exponents.reshape(2, 32, 8, 128),
        outer_params,
        outer_momentum,
        tensor_partials.reshape(TOK, D),
        residual_stream,
        norm_gain.reshape(64, 128),
    )
    return pl.pallas_call(
        hand_over,
        out_shape=out_shape,
        in_specs=[any_spec] * 3,
        out_specs=(any_spec,) * 3,
        scratch_shapes=[vmem(out.shape, out.dtype) for out in out_shape] + [pltpu.SemaphoreType.DMA((6,))],
        name="hand_over",
    )(*outs)


def solution(mesh):
    return jax.shard_map(
        per_device,
        mesh=mesh,
        in_specs=(
            P("replica", None, None, "tensor"),
            P("replica", None, None, "tensor"),
            P(None, "replica", "tensor"),
            P(None, "replica", "tensor"),
            P("tensor", "replica", None),
            P("replica", "tensor"),
            P(),
        ),
        out_specs=(
            P(None, "replica", "tensor"),
            P(None, "replica", "tensor"),
            P(None, "replica", "tensor"),
        ),
        check_vma=False,
    )
```

time: 116 us -> 92 us (0.79)
  the two profiles are of different devices: /device:TPU:25 before, /device:TPU:1 now
where the time goes in v2:
time: 92 us; the launch traced here: 91.9 us
  Pallas kernels  91.2 us (99%)
    pallas_call x1, Pallas kernels, per_device(): pl.pallas_call(kernel, out_shape=out_shape, in_specs=[any_spec] * 7, out_...  89.3 us
    pallas_call x1, Pallas kernels, per_device(): pl.pallas_call(hand_over, out_shape=out_shape, in_specs=[any_spec] * 3, o...  1.89 us

profile of v2, /device:TPU:1, one launch (start us, length us, event | category | flops | bytes accessed | tf_op | source)
XLA Modules:
  0.0 91.9 jit_solution(1414677241124822578)
XLA Ops:
  0.6 89.3 %outer_step.1 = (bf16[2,384,128]{2,1,0:T(8,128)(2,1)}, f32[2,256,128]{2,1,0:T(8,128)}, f32[2,256,128]{2,1,0:T(8,128)}) custom-call(s32[2,32,2,64,128]{4,3,2,1,0:T(8,128)} %bitcast.5, s32[2,32,8,128]{3,2,1,0:T(8,128)} %bitcast.6, f32[2,256,128]{2,1,0:T(8,128)} %params.1, f32[2,256,128]{2,1,0:T(8,128)} %momentum.1, bf16[384,8192]{1,0:T(8,128)(2,1)} %bitcast.4, ...), custom_call_target="tpu_custom_call" | custom-call | flops 1610612736 | bytes 13631488 | tf_op jit(solution)/shard_map/outer_step/pallas_call | solution.py:642
  90.0 1.9 %hand_over.1 = (bf16[2,384,128]{2,1,0:T(8,128)(2,1)}, f32[2,256,128]{2,1,0:T(8,128)}, f32[2,256,128]{2,1,0:T(8,128)}) custom-call(bf16[2,384,128]{2,1,0:T(8,128)(2,1)} %get-tuple-element.6.refs_0_, f32[2,256,128]{2,1,0:T(8,128)} %get-tuple-element.7.refs_1_, f32[2,256,128]{2,1,0:T(8,128)} %get-tuple-element.8.refs_2_), custom_call_target="tpu_custom_call" | custom-call | tf_op jit(solution)/shard_map/hand_over/pallas_call | solution.py:662

commit v3 on v2

--- a/solution.py
+++ b/solution.py
@@ -15,24 +15,24 @@
 outer_beta = 0.9
 norm_epsilon = 1e-05
 
-Y_FIRST = (0, 1, 2, 3, 4, 5, 6)
-X_FIRST = (7,)
-H_ORDER = (0, 7, 1, 2, 3, 4, 5, 6)
-
+Y_FIRST = (0, 1, 2, 4, 5, 6, 7)
+X_FIRST = (3,)
+H_ORDER = (0, 3, 1, 2, 4, 5, 6, 7)
+HALF = TOK // 2
 
 PLAN = {
     "other": (1.5, 3.7, 6.8, 10.0),
     "own": (3.0, 5.4, 7.5, 10.7),
     "pair": (4.9, 6.3, 9.6, 13.0),
-    "hop": 3.5,
-    "cross": 4.0,
-    "gather": (29.0, 37.0),
+    "hop": 3.0,
+    "cross": 4.2,
+    "greet": (6.0, 8.0, 10.0, 11.0),
+    "gather": (24.7, 29.7),
     "piece": 0.8,
     "relay": 4.0,
-    "start": (3.1, 3.2, 5.5, 10.5, 15.0, 19.0, 24.0, 29.0),
-    "y": (0.0, 7.0, 14.0, 19.0),
-    "x": (0.0, 10.0, 15.0, 20.0, 24.0),
-    "greet": (6.0, 9.0, 12.0, 14.0),
+    "start": (3.1, 3.2, 6.5, 10.5, 15.2, 19.9, 24.6, 29.3),
+    "y": (0.0, 8.0, 16.0, 23.0),
+    "x": (0.0, 11.0, 18.0, 24.0, 29.0),
     "squares": 8.0,
 }
 
@@ -53,7 +53,7 @@
 RECV = Slots()
 for _name, _count in (
     ("sib", 4), ("z", 4 * 2 * 4), ("xh", 4), ("a2a", 8), ("ag", 4 * 2 * 4), ("ya", 8 * 2), ("yb", 8 * 2),
-    ("yc", 8 * 2), ("xl", 8 * 2), ("asib", 8 * 2), ("ss", 4), ("p", 8),
+    ("yc", 8 * 2), ("xl", 8 * 2), ("asib", 8), ("ss", 4), ("p", 16),
 ):
     RECV.add(_name, _count)
 N_SEND = 256
@@ -148,16 +148,19 @@
     load_codes(0)
     exp_load = load(exps, ebuf, LOCAL["misc"])
     res_load = load(residual, rbuf, LOCAL["misc"] + 1)
-    load_part(H_ORDER[0])
+    first = [2 * (H_ORDER[0] % 4), 2 * (H_ORDER[0] % 4) + 1]
+    for k in first:
+        load_part(k)
     state_loads = []
 
     def more_loads():
-        load_part(H_ORDER[1])
         load_codes(1)
-        load_part(H_ORDER[2])
+        rest = [k for u in H_ORDER for k in (2 * (u % 4), 2 * (u % 4) + 1) if u < 4 and k not in first]
+        for k in rest[:2]:
+            load_part(k)
         load_codes(2)
         load_codes(3)
-        for k in H_ORDER[3:]:
+        for k in rest[2:]:
             load_part(k)
         state_loads.append(load(gain, gbuf, LOCAL["misc"] + 4))
         state_loads.append(load(params, pbuf, LOCAL["misc"] + 2))
@@ -275,7 +278,7 @@
         frag[q] = new_params.astype(BF16)
         y_to = 2 * c + half
         column = place_of(lax.rem(y - y_to + 4, 4))
-        slot = wbuf.at[z * 2 + xh, :, pl.ds(pl.multiple_of(128 * column, 128), 128)]
+        slot = wbuf.at[xh, z, :, pl.ds(pl.multiple_of(128 * column, 128), 128)]
         index = RECV["a2a"] + xh * 4 + column
         here = (c == j) & (y == y_to)
 
@@ -287,10 +290,10 @@
         send(frag.at[q], slot, index, dev(1 - xh, z, j, xl, y_to))
 
     def w_block(source_z, i):
-        return wbuf.at[pl.ds(source_z * 2, 2), :, pl.ds(128 * i, 128)]
+        return wbuf.at[:, source_z, :, pl.ds(128 * i, 128)]
 
     def w_half(source_z, a, i):
-        return wbuf.at[source_z * 2 + a, :, pl.ds(128 * i, 128)]
+        return wbuf.at[a, source_z, :, pl.ds(128 * i, 128)]
 
     def w_step(i, core, step):
         like = w_block(0, i) if step < 3 else w_half(0, 0, i)
@@ -317,80 +320,92 @@
     def lanes(x_, y_):
         return pl.ds(pl.multiple_of(128 * (x_ * 4 + y_), 128), 128)
 
-    def add_rows(out, rows, *terms):
-        @pl.loop(0, rows // 64)
-        def _(i):
-            at = pl.ds(pl.multiple_of(i * 64, 64), 64)
-            value = terms[0](at).astype(F32)
-            for term in terms[1:]:
-                value = value + term(at).astype(F32)
-            out(at, value)
-
-    def h_load(k):
-        part_loads[k].wait()
-        if k == H_ORDER[0]:
-            res_load.wait()
-
-        @pl.when(t == k)
-        def _():
-            @pl.loop(0, TOK // 16)
+    def add_rows(out, *terms):
+        for g in range(2):
+            @pl.loop(0, HALF // 64)
             def _(i):
-                at = pl.ds(pl.multiple_of(i * 16, 16), 16)
-                part[k, at, :] = (part[k, at, :].astype(F32) + rbuf[at, :].astype(F32)).astype(BF16)
-
-    def hy_start(k):
-        h_load(k)
-        n = Y_FIRST.index(k)
-        for d in range(2):
-            sign = 1 - 2 * d
-            send(part.at[k, :, lanes(d, yp(2))], yra.at[n, d], RECV["ya"] + k * 2 + d, y_next[d])
-        for d in range(2):
-            sign = 1 - 2 * d
-            send(part.at[k, :, lanes(1 - d, yp(sign))], yrb.at[n, d], RECV["yb"] + k * 2 + d, y_next[d])
-
-    def hy_middle(k):
-        n = Y_FIRST.index(k)
-        for d in range(2):
-            sign = 1 - 2 * d
-            wait_recv(yra.at[n, d], RECV["ya"] + k * 2 + d)
-            own = lanes(d, yp(sign))
-
-            def put(at, value, d=d):
-                yout[n, d, at, :] = value.astype(BF16)
-
-            add_rows(put, TOK, lambda at, own=own: part[k, at, own], lambda at, d=d: yra[n, d, at, :])
-            send(yout.at[n, d], yrc.at[n, d], RECV["yc"] + k * 2 + d, y_next[d])
-
-    def hy_cross(k):
-        n = Y_FIRST.index(k)
-        for d in range(2):
-            wait_recv(yrb.at[n, d], RECV["yb"] + k * 2 + d)
-            wait_recv(yrc.at[n, d], RECV["yc"] + k * 2 + d)
+                at = pl.multiple_of(i * 64, 64)
+                value = terms[0](g, at).astype(F32)
+                for term in terms[1:]:
+                    value = value + term(g, at).astype(F32)
+                out(g, at, value)
+
+    def rows(at):
+        return pl.ds(at, 64)
+
+    def tokens(u):
+        return pl.ds(HALF * (u // 4), HALF)
+
+    def groups(u):
+        return pl.ds(2 * (u % 4), 2)
+
+    def part_term(u, own):
+        return lambda g, at: part[2 * (u % 4) + g, pl.ds(HALF * (u // 4) + at, 64), own]
+
+    loaded = []
+
+    def h_load(u):
+        if u % 4 in loaded:
+            return
+        loaded.append(u % 4)
+        for k in (2 * (u % 4), 2 * (u % 4) + 1):
+            part_loads[k].wait()
+            if len(loaded) == 1 and k % 2 == 0:
+                res_load.wait()
+
+            @pl.when(t == k)
+            def _():
+                @pl.loop(0, TOK // 16)
+                def _(i):
+                    at = pl.ds(pl.multiple_of(i * 16, 16), 16)
+                    part[k, at, :] = (part[k, at, :].astype(F32) + rbuf[at, :].astype(F32)).astype(BF16)
+
+    def hy_start(u):
+        h_load(u)
+        for d in range(2):
+            send(part.at[groups(u), tokens(u), lanes(d, yp(2))], yra.at[u, d], RECV["ya"] + u * 2 + d, y_next[d])
+        for d in range(2):
+            piece = part.at[groups(u), tokens(u), lanes(1 - d, yp(1 - 2 * d))]
+            send(piece, yrb.at[u, d], RECV["yb"] + u * 2 + d, y_next[d])
+
+    def hy_middle(u):
+        for d in range(2):
+            wait_recv(yra.at[u, d], RECV["ya"] + u * 2 + d)
+
+            def put(g, at, value, d=d):
+                yout[u, d, g, rows(at), :] = value.astype(BF16)
+
+            add_rows(put, part_term(u, lanes(d, yp(1 - 2 * d))), lambda g, at, d=d: yra[u, d, g, rows(at), :])
+            send(yout.at[u, d], yrc.at[u, d], RECV["yc"] + u * 2 + d, y_next[d])
+
+    def hy_cross(u):
+        for d in range(2):
+            wait_recv(yrb.at[u, d], RECV["yb"] + u * 2 + d)
+            wait_recv(yrc.at[u, d], RECV["yc"] + u * 2 + d)
 
         for x_ in range(2):
-            own = lanes(x_, y)
-
-            def put(at, value, x_=x_):
-                xo[n, x_, at, :] = value.astype(BF16)
+            def put(g, at, value, x_=x_):
+                xo[u, x_, g, rows(at), :] = value.astype(BF16)
 
             add_rows(
-                put, TOK, lambda at, own=own: part[k, at, own], lambda at, x_=x_: yrb[n, 1 - x_, at, :],
-                lambda at, x_=x_: yrc[n, x_, at, :],
+                put, part_term(u, lanes(x_, y)), lambda g, at, x_=x_: yrb[u, 1 - x_, g, rows(at), :],
+                lambda g, at, x_=x_: yrc[u, x_, g, rows(at), :],
             )
-            send(xo.at[n, x_], xr.at[n, x_], RECV["xl"] + k * 2 + x_, x_pair)
-
-    def place_at(k, x_):
-        return pl.ds(pl.multiple_of(128 * (((2 * k) % 8) * 2 + 2 * x_ + k // 4), 128), 128)
-
-    def finish(k, x_, at, value):
+            send(xo.at[u, x_], xr.at[u, x_], RECV["xl"] + u * 2 + x_, x_pair)
+
+    def finish(u, x_, g, at, value):
+        k = 2 * (u % 4) + g
         hidden = value.astype(BF16).astype(F32)
         scaled = hidden * gbuf[pl.ds(8 * k + 4 * x_ + y, 1), :]
-        abuf[c, at, place_at(k, x_)] = scaled.astype(BF16)
-        ssacc[at, :] += hidden * hidden
-
-    def finished(k, x_):
-        piece = abuf.at[c, :, place_at(k, x_)]
-        send(piece, piece, RECV["asib"] + k * 2 + x_, sibling)
+        to = pl.ds(HALF * (u // 4) + at, 64)
+        abuf[c, to, pl.ds(pl.multiple_of(128 * (2 * k + x_), 128), 128)] = scaled.astype(BF16)
+        ssacc[to, :] += hidden * hidden
+
+    def unit_share(core, u):
+        return abuf.at[core, tokens(u), pl.ds(512 * (u % 4), 512)]
+
+    def finished(u):
+        send(unit_share(c, u), unit_share(c, u), RECV["asib"] + u, sibling)
 
     gain_waited = []
 
@@ -400,83 +415,72 @@
             ssacc[...] = jnp.zeros_like(ssacc)
             gain_waited.append(True)
 
-    def hy_end(k):
-        n = Y_FIRST.index(k)
+    def hy_end(u):
         gain_ready()
         for x_ in range(2):
-            wait_recv(xr.at[n, x_], RECV["xl"] + k * 2 + x_)
+            wait_recv(xr.at[u, x_], RECV["xl"] + u * 2 + x_)
             add_rows(
-                lambda at, value, x_=x_: finish(k, x_, at, value), TOK,
-                lambda at, x_=x_: xo[n, x_, at, :], lambda at, x_=x_: xr[n, x_, at, :],
+                lambda g, at, value, x_=x_: finish(u, x_, g, at, value),
+                lambda g, at, x_=x_: xo[u, x_, g, rows(at), :], lambda g, at, x_=x_: xr[u, x_, g, rows(at), :],
             )
-            finished(k, x_)
-
-    def hx_start(k):
-        h_load(k)
-        n = X_FIRST.index(k)
+        finished(u)
+
+    def hx_start(u):
+        h_load(u)
         other = pl.ds(pl.multiple_of(512 * (1 - xl), 512), 512)
-        send(part.at[k, :, other], xr4.at[n], RECV["xl"] + k * 2, x_pair)
-
-    half_rows = (pl.ds(0, 192), pl.ds(192, 192))
+        send(part.at[groups(u), tokens(u), other], xr4.at[X_FIRST.index(u)], RECV["xl"] + u * 2, x_pair)
 
     def hx_lanes(y_):
         return pl.ds(pl.multiple_of(128 * y_, 128), 128)
 
-    def hx_cross(k):
-        n = X_FIRST.index(k)
-        wait_recv(xr4.at[n], RECV["xl"] + k * 2)
+    def hx_cross(u):
+        n = X_FIRST.index(u)
+        wait_recv(xr4.at[n], RECV["xl"] + u * 2)
         own = pl.ds(pl.multiple_of(512 * xl, 512), 512)
 
-        @pl.loop(0, TOK // 16)
-        def _(i):
-            at = pl.ds(pl.multiple_of(i * 16, 16), 16)
-            xs[n, at, :] = (part[k, at, own].astype(F32) + xr4[n, at, :].astype(F32)).astype(BF16)
-
-        for d in range(2):
-            send(
-                xs.at[n, half_rows[d], hx_lanes(yp(2))], yra.at[len(Y_FIRST) + n, d, pl.ds(0, 192)],
-                RECV["ya"] + k * 2 + d, y_next[d],
-            )
-
-    def hx_middle(k):
-        n = X_FIRST.index(k)
-        m = len(Y_FIRST) + n
-        for d in range(2):
-            sign = 1 - 2 * d
-            wait_recv(yra.at[m, d, pl.ds(0, 192)], RECV["ya"] + k * 2 + d)
-            own = hx_lanes(yp(sign))
-
-            @pl.loop(0, 192 // 64)
+        def put(g, at, value):
+            xs[n, g, rows(at), :] = value.astype(BF16)
+
+        add_rows(put, part_term(u, own), lambda g, at: xr4[n, g, rows(at), :])
+        for d in range(2):
+            send(xs.at[n, d, :, hx_lanes(yp(2))], yra.at[u, d, 0], RECV["ya"] + u * 2 + d, y_next[d])
+
+    def hx_middle(u):
+        n = X_FIRST.index(u)
+        for d in range(2):
+            wait_recv(yra.at[u, d, 0], RECV["ya"] + u * 2 + d)
+            own = hx_lanes(yp(1 - 2 * d))
+
+            @pl.loop(0, HALF // 64)
             def _(i, d=d, own=own):
-                at = pl.ds(pl.multiple_of(192 * d + i * 64, 64), 64)
-                got = pl.ds(pl.multiple_of(i * 64, 64), 64)
-                xs[n, at, own] = (xs[n, at, own].astype(F32) + yra[m, d, got, :].astype(F32)).astype(BF16)
-
-            send(xs.at[n, :, own], yrc.at[m, d], RECV["yc"] + k * 2 + d, y_next[d])
-
-    def hx_end(k):
-        n = X_FIRST.index(k)
-        m = len(Y_FIRST) + n
+                at = rows(pl.multiple_of(i * 64, 64))
+                xs[n, d, at, own] = (xs[n, d, at, own].astype(F32) + yra[u, d, 0, at, :].astype(F32)).astype(BF16)
+
+            send(xs.at[n, :, :, own], yrc.at[u, d], RECV["yc"] + u * 2 + d, y_next[d])
+
+    def hx_end(u):
+        n = X_FIRST.index(u)
         gain_ready()
         for d in range(2):
-            wait_recv(yrc.at[m, d], RECV["yc"] + k * 2 + d)
+            wait_recv(yrc.at[u, d], RECV["yc"] + u * 2 + d)
         own = hx_lanes(y)
 
-        def put(at, value):
-            xo[m, 0, at, :] = value.astype(BF16)
-            finish(k, xl, at, value)
+        def put(g, at, value):
+            xo[u, 0, g, rows(at), :] = value.astype(BF16)
+            finish(u, xl, g, at, value)
 
         add_rows(
-            put, TOK, lambda at: xs[n, at, own], lambda at: yrc[m, 0, at, :], lambda at: yrc[m, 1, at, :]
+            put, lambda g, at: xs[n, g, rows(at), own], lambda g, at: yrc[u, 0, g, rows(at), :],
+            lambda g, at: yrc[u, 1, g, rows(at), :],
         )
-        send(xo.at[m, 0], xr.at[m, 0], RECV["xl"] + k * 2 + 1, x_pair)
-        finished(k, xl)
-
-    def hx_last(k):
-        m = len(Y_FIRST) + X_FIRST.index(k)
-        wait_recv(xr.at[m, 0], RECV["xl"] + k * 2 + 1)
-        add_rows(lambda at, value: finish(k, 1 - xl, at, value), TOK, lambda at: xr[m, 0, at, :])
-        finished(k, 1 - xl)
+        send(xo.at[u, 0], xr.at[u, 0], RECV["xl"] + u * 2 + 1, x_pair)
+
+    def hx_last(u):
+        wait_recv(xr.at[u, 0], RECV["xl"] + u * 2 + 1)
+        add_rows(
+            lambda g, at, value: finish(u, 1 - xl, g, at, value), lambda g, at: xr[u, 0, g, rows(at), :]
+        )
+        finished(u)
 
     def ss_send():
         for b in range(3):
@@ -495,37 +499,41 @@
             block = jnp.broadcast_to(inverse[0:1, 128 * b : 128 * b + 128], (128, 128))
             invb[pl.ds(128 * b, 128), :] = block.T
 
-    def hidden_ready():
-        for k in range(8):
-            for x_ in range(2):
-                wait_recv(abuf.at[1 - c, :, place_at(k, x_)], RECV["asib"] + k * 2 + x_)
-
-    pout_like = pout.at[0, 0]
-
-    def project(i, core):
+    def hidden_ready(th):
+        for u in range(4 * th, 4 * th + 4):
+            wait_recv(unit_share(1 - c, u), RECV["asib"] + u)
+
+    pout_like = pout.at[0, 0, pl.ds(0, HALF)]
+
+    def project(i, core, th):
         mine = c == core
+        at = pl.ds(HALF * th, HALF)
 
         @pl.when(mine)
         def _():
-            w = wbuf[:, :, pl.ds(128 * i, 128)].reshape(2048, 128)
+            w = wbuf[:, :, :, pl.ds(128 * i, 128)].reshape(2048, 128)
+            a = abuf[:, at, :].reshape(2 * HALF, 2048)
+            products = jnp.dot(a, w, preferred_element_type=F32).astype(BF16)
             for b in range(2):
-                pout[i, b] = jnp.dot(abuf[b], w, preferred_element_type=F32).astype(BF16)
-                slot = precv.at[core, y]
-                index = RECV["p"] + core * 4 + y
+                pout[i, b, at, :] = products[b * HALF : b * HALF + HALF]
+            for b in range(2):
+                piece = pout.at[i, b, at]
+                slot = precv.at[core, y, at]
+                index = RECV["p"] + (core * 4 + y) * 2 + th
                 if away[i] == 0 and b == core:
-                    pltpu.make_async_copy(pout.at[i, b], slot, rsem.at[index]).start()
+                    pltpu.make_async_copy(piece, slot, rsem.at[index]).start()
                 else:
                     device = dev(xh, z, b, xl, yp(away[i]))
-                    send(pout.at[i, b], slot, index, device, inside=mine, like=pout_like)
-
-    def result():
+                    send(piece, slot, index, device, inside=mine, like=pout_like)
+
+    def result(th):
         for j in range(2):
             for source in range(4):
-                wait_recv(precv.at[j, source], RECV["p"] + j * 4 + source)
-
-            @pl.loop(0, TOK // 32)
+                wait_recv(precv.at[j, source, pl.ds(HALF * th, HALF)], RECV["p"] + (j * 4 + source) * 2 + th)
+
+            @pl.loop(0, HALF // 32)
             def _(i):
-                at = pl.ds(pl.multiple_of(i * 32, 32), 32)
+                at = pl.ds(pl.multiple_of(HALF * th + i * 32, 32), 32)
                 value = precv[j, 0, at, :].astype(F32)
                 for source in range(1, 4):
                     value = value + precv[j, source, at, :].astype(F32)
@@ -540,27 +548,32 @@
             task(base + PLAN["hop"] * (step - 1), g_ring, q, step)
         task(base + PLAN["hop"] * 4, g_final, q)
         task(base + PLAN["hop"] * 4 + PLAN["cross"], g_update, q)
-    for n, k in enumerate(H_ORDER):
+        task(PLAN["greet"][q], greet, q + 1)
+    ready = [0.0, 0.0]
+    for n, u in enumerate(H_ORDER):
         start = PLAN["start"][n]
-        if k in Y_FIRST:
-            for function, after in zip((hy_start, hy_middle, hy_cross, hy_end), PLAN["y"]):
-                task(start + after, function, k)
+        if u in Y_FIRST:
+            steps = zip((hy_start, hy_middle, hy_cross, hy_end), PLAN["y"])
         else:
-            for function, after in zip((hx_start, hx_cross, hx_middle, hx_end, hx_last), PLAN["x"]):
-                task(start + after, function, k)
-    hidden_time = max(item[0] for item in tasks if item[2] in (hy_end, hx_last))
-    task(hidden_time + 0.01, ss_send)
-    task(hidden_time + 0.02, hidden_ready)
-    task(hidden_time + PLAN["squares"], ss_receive)
+            steps = zip((hx_start, hx_cross, hx_middle, hx_end, hx_last), PLAN["x"])
+        for function, after in steps:
+            task(start + after, function, u)
+            ready[u // 4] = max(ready[u // 4], start + after)
+    ready[1] = max(ready) + 0.01
+    for th in range(2):
+        task(ready[th] + 0.5, hidden_ready, th)
+    task(ready[1] + 0.3, ss_send)
     for core in range(2):
         for i in range(4):
             base = PLAN["gather"][core] + PLAN["piece"] * i
             for step in range(5):
                 task(base + PLAN["relay"] * step, w_step, i, core, step)
-            task(max(base + PLAN["relay"] * 4, hidden_time) + 0.1, project, i, core)
-    for stage, time in zip((1, 2, 3, 4), PLAN["greet"]):
-        task(time, greet, stage)
-    task(1000.0, result)
+            for th in range(2):
+                task(max(base + PLAN["relay"] * 4, ready[th] + 0.5) + 0.1, project, i, core, th)
+    end = max(item[0] for item in tasks)
+    task(ready[1] + PLAN["squares"], ss_receive)
+    task(max(end, ready[1] + PLAN["squares"]) + 1.0, result, 0)
+    task(max(end, ready[1] + PLAN["squares"]) + 2.0, result, 1)
     outs = []
     for _, _, function, arguments in sorted(tasks, key=lambda item: item[:2]):
         function(*arguments)
@@ -590,7 +603,7 @@
 def per_device(
     delta_codes, scale_exponents, outer_params, outer_momentum, tensor_partials, residual_stream, norm_gain
 ):
-    ny, nx = len(Y_FIRST), len(X_FIRST)
+    nx = max(len(X_FIRST), 1)
     vmem = pltpu.VMEM
     scratch = [
         vmem((4, 32, 64, 128), jnp.int32),
@@ -610,16 +623,16 @@
         vmem((2, 256, 128), F32),
         vmem((2, 256, 128), F32),
         vmem((4, 128, 128), BF16),
-        vmem((16, 128, 512), BF16),
+        vmem((2, 8, 128, 512), BF16),
         vmem((8, TOK, 1024), BF16),
-        vmem((8, 2, TOK, 128), BF16),
-        vmem((ny, 2, TOK, 128), BF16),
-        vmem((8, 2, TOK, 128), BF16),
-        vmem((ny, 2, TOK, 128), BF16),
-        vmem((8, 2, TOK, 128), BF16),
-        vmem((8, 2, TOK, 128), BF16),
-        vmem((nx, TOK, 512), BF16),
-        vmem((nx, TOK, 512), BF16),
+        vmem((8, 2, 2, HALF, 128), BF16),
+        vmem((8, 2, 2, HALF, 128), BF16),
+        vmem((8, 2, 2, HALF, 128), BF16),
+        vmem((8, 2, 2, HALF, 128), BF16),
+        vmem((8, 2, 2, HALF, 128), BF16),
+        vmem((8, 2, 2, HALF, 128), BF16),
+        vmem((nx, 2, HALF, 512), BF16),
+        vmem((nx, 2, HALF, 512), BF16),
         vmem((2, TOK, 2048), BF16),
         vmem((TOK, 128), F32),
         vmem((8, TOK), F32),

time: 92 us -> 88.8 us (0.965)
  Pallas kernels: 91.2 us -> 88.1 us
    pallas_call x1, Pallas kernels: 89.3 us -> 86.2 us  [per_device(): pl.pallas_call(kernel, out_shape=out_shape, in_specs=[any_spec] * 7, out_...]
where the time goes in v3:
time: 88.8 us; the launch traced here: 88.7 us
  Pallas kernels  88.1 us (99%)
    pallas_call x1, Pallas kernels, per_device(): pl.pallas_call(kernel, out_shape=out_shape, in_specs=[any_spec] * 7, out_...  86.2 us
    pallas_call x1, Pallas kernels, per_device(): pl.pallas_call(hand_over, out_shape=out_shape, in_specs=[any_spec] * 3, o...  1.89 us

profile of v3, /device:TPU:1, one launch (start us, length us, event | category | flops | bytes accessed | tf_op | source)
XLA Modules:
  0.0 88.7 jit_solution(11118264341047350155)
XLA Ops:
  0.6 86.2 %outer_step.1 = (bf16[2,384,128]{2,1,0:T(8,128)(2,1)}, f32[2,256,128]{2,1,0:T(8,128)}, f32[2,256,128]{2,1,0:T(8,128)}) custom-call(s32[2,32,2,64,128]{4,3,2,1,0:T(8,128)} %bitcast.5, s32[2,32,8,128]{3,2,1,0:T(8,128)} %bitcast.6, f32[2,256,128]{2,1,0:T(8,128)} %params.1, f32[2,256,128]{2,1,0:T(8,128)} %momentum.1, bf16[384,8192]{1,0:T(8,128)(2,1)} %bitcast.4, ...), custom_call_target="tpu_custom_call" | custom-call | flops 1610612736 | bytes 13631488 | tf_op jit(solution)/shard_map/outer_step/pallas_call | solution.py:655
  86.8 1.9 %hand_over.1 = (bf16[2,384,128]{2,1,0:T(8,128)(2,1)}, f32[2,256,128]{2,1,0:T(8,128)}, f32[2,256,128]{2,1,0:T(8,128)}) custom-call(bf16[2,384,128]{2,1,0:T(8,128)(2,1)} %get-tuple-element.6.refs_0_, f32[2,256,128]{2,1,0:T(8,128)} %get-tuple-element.7.refs_1_, f32[2,256,128]{2,1,0:T(8,128)} %get-tuple-element.8.refs_2_), custom_call_target="tpu_custom_call" | custom-call | tf_op jit(solution)/shard_map/hand_over/pallas_call | solution.py:675

commit v4 on v3

--- a/solution.py
+++ b/solution.py
@@ -27,8 +27,8 @@
     "hop": 3.0,
     "cross": 4.2,
     "greet": (6.0, 8.0, 10.0, 11.0),
-    "gather": (24.7, 29.7),
-    "piece": 0.8,
+    "gather": (23.2, 29.7),
+    "piece": 0.9,
     "relay": 4.0,
     "start": (3.1, 3.2, 6.5, 10.5, 15.2, 19.9, 24.6, 29.3),
     "y": (0.0, 8.0, 16.0, 23.0),
@@ -575,14 +575,27 @@
     task(max(end, ready[1] + PLAN["squares"]) + 1.0, result, 0)
     task(max(end, ready[1] + PLAN["squares"]) + 2.0, result, 1)
     outs = []
+    drained = 0
+
+    def drain(limit, most):
+        count = max(0, min(most, limit - drained))
+        for index in range(drained, drained + count):
+            wait_send(index)
+        return drained + count
+
     for _, _, function, arguments in sorted(tasks, key=lambda item: item[:2]):
+        if function is result and arguments == (0,):
+            drained = drain(len(sends) - 16, len(sends))
         function(*arguments)
         if function is g_update and arguments == (3,):
             outs.append(load(newp, params_out, LOCAL["out"]))
             outs.append(load(newm, momentum_out, LOCAL["out"] + 1))
-    outs.append(load(kvbuf, kv_out, LOCAL["out"] + 2))
-    for index in range(len(sends)):
-        wait_send(index)
+        if function is result:
+            half = pl.ds(HALF * arguments[0], HALF)
+            outs.append(load(kvbuf.at[:, half], kv_out.at[:, half], LOCAL["out"] + 2 + arguments[0]))
+        else:
+            drained = drain(len(sends) - 48, 6)
+    drained = drain(len(sends), len(sends))
     for copy in outs:
         copy.wait()
 

time: 88.8 us -> 87.8 us (0.989)
  Pallas kernels: 88.1 us -> 87.1 us
    pallas_call x1, Pallas kernels: 86.2 us -> 85.2 us  [per_device(): pl.pallas_call(kernel, out_shape=out_shape, in_specs=[any_spec] * 7, out_...]
where the time goes in v4:
time: 87.8 us; the launch traced here: 87.7 us
  Pallas kernels  87.1 us (99%)
    pallas_call x1, Pallas kernels, per_device(): pl.pallas_call(kernel, out_shape=out_shape, in_specs=[any_spec] * 7, out_...  85.2 us
    pallas_call x1, Pallas kernels, per_device(): pl.pallas_call(hand_over, out_shape=out_shape, in_specs=[any_spec] * 3, o...  1.89 us

profile of v4, /device:TPU:1, one launch (start us, length us, event | category | flops | bytes accessed | tf_op | source)
XLA Modules:
  0.0 87.7 jit_solution(1150165470524962741)
XLA Ops:
  0.6 85.2 %outer_step.1 = (bf16[2,384,128]{2,1,0:T(8,128)(2,1)}, f32[2,256,128]{2,1,0:T(8,128)}, f32[2,256,128]{2,1,0:T(8,128)}) custom-call(s32[2,32,2,64,128]{4,3,2,1,0:T(8,128)} %bitcast.5, s32[2,32,8,128]{3,2,1,0:T(8,128)} %bitcast.6, f32[2,256,128]{2,1,0:T(8,128)} %params.1, f32[2,256,128]{2,1,0:T(8,128)} %momentum.1, bf16[384,8192]{1,0:T(8,128)(2,1)} %bitcast.4, ...), custom_call_target="tpu_custom_call" | custom-call | flops 1610612736 | bytes 13631488 | tf_op jit(solution)/shard_map/outer_step/pallas_call | solution.py:668
  85.8 1.9 %hand_over.1 = (bf16[2,384,128]{2,1,0:T(8,128)(2,1)}, f32[2,256,128]{2,1,0:T(8,128)}, f32[2,256,128]{2,1,0:T(8,128)}) custom-call(bf16[2,384,128]{2,1,0:T(8,128)(2,1)} %get-tuple-element.6.refs_0_, f32[2,256,128]{2,1,0:T(8,128)} %get-tuple-element.7.refs_1_, f32[2,256,128]{2,1,0:T(8,128)} %get-tuple-element.8.refs_2_), custom_call_target="tpu_custom_call" | custom-call | tf_op jit(solution)/shard_map/hand_over/pallas_call | solution.py:688

commit v5 on v4

--- a/solution.py
+++ b/solution.py
@@ -255,10 +255,10 @@
         send(xout.at[q], xrecv.at[q], RECV["xh"] + q, xh_pair)
         fin[q] = total(xh)
 
-    away = (2, 1, 3, 0)
+    away = (1, 3, 2, 0)
 
     def place_of(delta):
-        return jnp.where(delta == 2, 0, jnp.where(delta == 1, 1, jnp.where(delta == 3, 2, 3)))
+        return jnp.where(delta == 1, 0, jnp.where(delta == 3, 1, jnp.where(delta == 2, 2, 3)))
 
     def g_update(q):
         j, half = q // 2, q % 2

time: 87.8 us -> 88.7 us (1.010)
  no operation moved by 1% of the time
where the time goes in v5:
time: 88.7 us; the launch traced here: 88.6 us
  Pallas kernels  87.9 us (99%)
    pallas_call x1, Pallas kernels, per_device(): pl.pallas_call(kernel, out_shape=out_shape, in_specs=[any_spec] * 7, out_...  86.1 us
    pallas_call x1, Pallas kernels, per_device(): pl.pallas_call(hand_over, out_shape=out_shape, in_specs=[any_spec] * 3, o...  1.89 us

profile of v5, /device:TPU:1, one launch (start us, length us, event | category | flops | bytes accessed | tf_op | source)
XLA Modules:
  0.0 88.6 jit_solution(3648936441092060256)
XLA Ops:
  0.6 86.1 %outer_step.1 = (bf16[2,384,128]{2,1,0:T(8,128)(2,1)}, f32[2,256,128]{2,1,0:T(8,128)}, f32[2,256,128]{2,1,0:T(8,128)}) custom-call(s32[2,32,2,64,128]{4,3,2,1,0:T(8,128)} %bitcast.5, s32[2,32,8,128]{3,2,1,0:T(8,128)} %bitcast.6, f32[2,256,128]{2,1,0:T(8,128)} %params.1, f32[2,256,128]{2,1,0:T(8,128)} %momentum.1, bf16[384,8192]{1,0:T(8,128)(2,1)} %bitcast.4, ...), custom_call_target="tpu_custom_call" | custom-call | flops 1610612736 | bytes 13631488 | tf_op jit(solution)/shard_map/outer_step/pallas_call | solution.py:668
  86.7 1.9 %hand_over.1 = (bf16[2,384,128]{2,1,0:T(8,128)(2,1)}, f32[2,256,128]{2,1,0:T(8,128)}, f32[2,256,128]{2,1,0:T(8,128)}) custom-call(bf16[2,384,128]{2,1,0:T(8,128)(2,1)} %get-tuple-element.6.refs_0_, f32[2,256,128]{2,1,0:T(8,128)} %get-tuple-element.7.refs_1_, f32[2,256,128]{2,1,0:T(8,128)} %get-tuple-element.8.refs_2_), custom_call_target="tpu_custom_call" | custom-call | tf_op jit(solution)/shard_map/hand_over/pallas_call | solution.py:688
